TPU v7x, 512 devices: a whole 4x4x16 slice. The times are simulated.
512 devices in a mesh: group: 8 (over x, z_hi), fsdp: 64 (over z_lo, y, core).
Axes of the slice: x: 4, y: 4, z: 16 (z_hi: 2, z_lo: 8; z = z_hi * 8 + z_lo), core: 2. Of those that a mesh axis runs over, the one named last changes fastest.
Arguments:
- hidden: bfloat16 [131072, 2304], P(('group', 'fsdp')), may hold values from -6 to 6
- grad_values: bfloat16 [131072, 1024], P(('group', 'fsdp')), may hold values from -6 to 6
- weights: float32 [8, 2304, 1024], P('group', 'fsdp'), may hold values from -6 to 6
- gains: float32 [8, 2304], P('group', 'fsdp'), may hold values from 0.5 to 1.5
- snapshot: float32 [8, 2304, 128], P('group', 'fsdp'), may hold values from -6 to 6
- outer_frag: float32 [2304, 128], P('fsdp'), may hold values from -6 to 6
- outer_moment: float32 [2304, 128], P('fsdp'), may hold values from -6 to 6
- fragment_index: int32 [1], replicated, may hold values from 0 to 7
Outputs:
- values: bfloat16 [131072, 1024], P(('group', 'fsdp'))
- grad_hidden: bfloat16 [131072, 2304], P(('group', 'fsdp'))
- new_weights: float32 [8, 2304, 1024], P('group', 'fsdp')
- new_gains: float32 [8, 2304], P('group', 'fsdp')
- new_outer: float32 [2304, 128], P('fsdp')
- new_moment: float32 [2304, 128], P('fsdp')
All inputs are finite; a program needn't handle non-finite values.
Results may differ from a plain program's by a relative error of at most 0.0015.
The roundings to bfloat16 on the way count: a program that leaves them out, or rounds other values in their place, can miss the bound.
Values may be sent and summed in bfloat16 or wider, within the bound.
A program may use at most 128 MiB of HBM per device.

v0:
```python
import jax
import jax.numpy as jnp
from jax import lax
from jax.sharding import PartitionSpec as P

D = 2304
KV = 1024
HEAD = 128


epsilon = 1e-06
inner_rate = 0.05
gain_rate = 0.002
momentum = 0.9
outer_rate = 0.7
mixing = 0.5


def outer_step(outer_cols, moment_cols, summed, workers):
    change = outer_cols - summed / workers
    moment_next = momentum * moment_cols + change
    outer_next = outer_cols - outer_rate * (change + momentum * moment_next)
    return (outer_next, moment_next)


def synchronise(snapshot, outer_frag, outer_moment):
    workers = float(lax.axis_size("group"))
    summed = lax.psum(snapshot[0], "group")
    return outer_step(outer_frag, outer_moment, summed, workers)


def weight_gradient(normed_bf, grad_values, factor):
    devices = lax.axis_size("fsdp")
    pieces = []
    for head_index in range(KV // HEAD):
        cotangent = grad_values[:, head_index * HEAD : (head_index + 1) * HEAD]
        partial_sum = (
            lax.dot_general(
                normed_bf, cotangent, (((0,), (0,)), ((), ())), preferred_element_type=jnp.float32
            )
            * factor
        )
        partial_sum = partial_sum.reshape(devices, partial_sum.shape[0] // devices, HEAD)
        received = lax.all_to_all(
            partial_sum.astype(jnp.bfloat16), "fsdp", split_axis=0, concat_axis=0, tiled=True
        ).astype(partial_sum.dtype)
        pieces.append(jnp.sum(received, axis=0))
    return jnp.concatenate(pieces, axis=1)


def body(hidden, grad_values, weights, gains, snapshot, outer_frag, outer_moment, fragment_index):
    factor = D ** (-0.5)
    weight_bf, gain_bf = (
        lax.all_gather(weights[0].astype(jnp.bfloat16), "fsdp", axis=0, tiled=True),
        lax.all_gather(gains[0].astype(jnp.bfloat16), "fsdp", axis=0, tiled=True),
    )
    tokens = hidden.astype(jnp.float32)
    inverse = lax.rsqrt(jnp.mean(tokens * tokens, axis=-1, keepdims=True) + epsilon)
    normed = tokens * inverse
    gain_wide = gain_bf.astype(jnp.float32)
    normed_bf = (normed * gain_wide).astype(jnp.bfloat16)
    values = (jnp.dot(normed_bf, weight_bf, preferred_element_type=jnp.float32) * factor).astype(
        jnp.bfloat16
    )
    input_grad = (
        lax.dot_general(
            grad_values, weight_bf, (((1,), (1,)), ((), ())), preferred_element_type=jnp.float32
        )
        * factor
    )
    weight_grad = weight_gradient(normed_bf, grad_values, factor)
    gain_grad = lax.psum_scatter(
        jnp.sum(input_grad * normed, axis=0), "fsdp", scatter_dimension=0, tiled=True
    )
    scaled = input_grad * gain_wide
    grad_hidden = (
        inverse * (scaled - normed * jnp.mean(scaled * normed, axis=-1, keepdims=True))
    ).astype(jnp.bfloat16)
    inner = weights[0] - inner_rate * weight_grad
    new_gains = gains[0] - gain_rate * gain_grad
    new_outer, new_moment = synchronise(snapshot, outer_frag, outer_moment)
    offset = fragment_index[0] * new_outer.shape[1]
    old_cols = lax.dynamic_slice_in_dim(inner, offset, new_outer.shape[1], 1)
    mixed_cols = mixing * old_cols + (1.0 - mixing) * new_outer
    new_weights = lax.dynamic_update_slice_in_dim(inner, mixed_cols, offset, 1)
    return (values, grad_hidden, new_weights[None], new_gains[None], new_outer, new_moment)


def solution(mesh):
    return jax.shard_map(
        body,
        mesh=mesh,
        in_specs=(
            P(("group", "fsdp"), None),
            P(("group", "fsdp"), None),
            P("group", "fsdp", None),
            P("group", "fsdp"),
            P("group", "fsdp", None),
            P("fsdp", None),
            P("fsdp", None),
            P(),
        ),
        out_specs=(
            P(("group", "fsdp"), None),
            P(("group", "fsdp"), None),
            P("group", "fsdp", None),
            P("group", "fsdp"),
            P("fsdp", None),
            P("fsdp", None),
        ),
        check_vma=False,
    )
```

profile of v0, /device:TPU:1, one launch (start us, length us, event | category | flops | bytes accessed | tf_op | source)
XLA Modules:
  0.0 1073.4 jit_solution(6526107761631290068)
XLA Ops:
  10.1 218.7 %all-reduce = bf16[2304]{0:T(1024)(128)(2,1)S(1)} all-reduce(bf16[2304]{0:T(1024)(128)(2,1)S(1)} %dynamic-update-slice), channel_id=1, replica_groups=mesh['group'=8,'fsdp'=64] {'fsdp'}, use_global_device_ids=true, to_apply=%add | all-reduce | flops 2304 | bytes 9216
  230.4 2.0 fusion
  233.3 12.5 %all-to-all-start = ((bf16[64,36,128]{2,1,0:T(8,128)(2,1)}), bf16[64,36,128]{2,1,0:T(8,128)(2,1)S(1)}, u32[]{:S(2)}, u32[]{:S(2)}) async-start(bf16[64,36,128]{2,1,0:T(8,128)(2,1)} %convert_element_type.101), calls=%async_computation | async-start | bytes 1310720 | tf_op jit(solution)/shard_map/all_to_all | solution.py:44
  248.3 33.1 %all-to-all-done = bf16[64,36,128]{2,1,0:T(8,128)(2,1)S(1)} async-done(((bf16[64,36,128]{2,1,0:T(8,128)(2,1)}), bf16[64,36,128]{2,1,0:T(8,128)(2,1)S(1)}, u32[]{:S(2)}, u32[]{:S(2)}) %all-to-all-start) | async-done | bytes 589856 | tf_op jit(solution)/shard_map/all_to_all | solution.py:44
  281.4 7.0 all-to-all-start.1
  290.8 33.0 %all-to-all-done.1 = bf16[64,36,128]{2,1,0:T(8,128)(2,1)S(1)} async-done(((bf16[64,36,128]{2,1,0:T(8,128)(2,1)}), bf16[64,36,128]{2,1,0:T(8,128)(2,1)S(1)}, u32[]{:S(2)}, u32[]{:S(2)}) %all-to-all-start.1) | async-done | bytes 589856 | tf_op jit(solution)/shard_map/all_to_all | solution.py:44
  323.8 7.0 all-to-all-start.2
  330.8 2.3 fusion.3
  333.1 2.0 convert_element_type.110
  335.1 31.1 %all-to-all-done.2 = bf16[64,36,128]{2,1,0:T(8,128)(2,1)S(1)} async-done(((bf16[64,36,128]{2,1,0:T(8,128)(2,1)}), bf16[64,36,128]{2,1,0:T(8,128)(2,1)S(1)}, u32[]{:S(2)}, u32[]{:S(2)}) %all-to-all-start.2) | async-done | bytes 589856 | tf_op jit(solution)/shard_map/all_to_all | solution.py:44
  366.2 7.2 all-to-all-start.3
  373.4 2.3 fusion.4
  375.7 2.0 convert_element_type.113
  377.7 31.1 %all-to-all-done.3 = bf16[64,36,128]{2,1,0:T(8,128)(2,1)} async-done(((bf16[64,36,128]{2,1,0:T(8,128)(2,1)}), bf16[64,36,128]{2,1,0:T(8,128)(2,1)}, u32[]{:S(2)}, u32[]{:S(2)}) %all-to-all-start.3) | async-done | bytes 589856 | tf_op jit(solution)/shard_map/all_to_all | solution.py:44
  408.8 7.2 all-to-all-start.4
  416.0 2.3 fusion.5
  418.3 2.0 convert_element_type.116
  420.3 31.0 %all-to-all-done.4 = bf16[64,36,128]{2,1,0:T(8,128)(2,1)} async-done(((bf16[64,36,128]{2,1,0:T(8,128)(2,1)}), bf16[64,36,128]{2,1,0:T(8,128)(2,1)}, u32[]{:S(2)}, u32[]{:S(2)}) %all-to-all-start.4) | async-done | bytes 589856 | tf_op jit(solution)/shard_map/all_to_all | solution.py:44
  451.3 7.2 all-to-all-start.5
  459.2 2.3 fusion.6
  463.5 32.5 %all-to-all-done.5 = bf16[64,36,128]{2,1,0:T(8,128)(2,1)} async-done(((bf16[64,36,128]{2,1,0:T(8,128)(2,1)}), bf16[64,36,128]{2,1,0:T(8,128)(2,1)}, u32[]{:S(2)}, u32[]{:S(2)}) %all-to-all-start.5) | async-done | bytes 589856 | tf_op jit(solution)/shard_map/all_to_all | solution.py:44
  496.0 5.2 all-to-all-start.6
  501.3 2.3 fusion.7
  503.6 2.0 convert_element_type.122
  505.6 35.5 %all-to-all-done.6 = bf16[64,36,128]{2,1,0:T(8,128)(2,1)} async-done(((bf16[64,36,128]{2,1,0:T(8,128)(2,1)}), bf16[64,36,128]{2,1,0:T(8,128)(2,1)}, u32[]{:S(2)}, u32[]{:S(2)}) %all-to-all-start.6) | async-done | bytes 589856 | tf_op jit(solution)/shard_map/all_to_all | solution.py:44
  541.1 6.9 all-to-all-start.7
  549.3 72.4 %psum.7 = f32[36,128]{1,0:T(8,128)S(1)} all-reduce(f32[36,128]{1,0:T(8,128)S(1)} %bitcast.44), channel_id=1, replica_groups=mesh['group'=8,'fsdp'=64] {'group'}, use_global_device_ids=true, to_apply=%region_10.0 | all-reduce | flops 4608 | bytes 36864 | tf_op jit(solution)/shard_map/psum | solution.py:28
  630.0 7.2 reshape.156
  637.2 4.7 fusion.19
  641.9 2.4 fusion.17
  644.9 418.1 %all-reduce.1 = f32[2304]{0:T(1024)} all-reduce(f32[2304]{0:T(1024)} %get-tuple-element.24), channel_id=2, replica_groups=mesh['group'=8,'fsdp'=64] {'fsdp'}, use_global_device_ids=true, to_apply=%region_12.0.clone | all-reduce | flops 2304 | bytes 18432
  1063.0 2.3 fusion.16
  (65 shorter events, 22.2 us)
Async XLA Ops:
  230.4 15.5 %copy-start = (bf16[256,2304]{1,0:T(8,128)(2,1)S(1)}, bf16[256,2304]{1,0:T(8,128)(2,1)}, u32[]{:S(2)}) copy-start(bf16[256,2304]{1,0:T(8,128)(2,1)} %param.8) | copy-start | bytes 3538948
  233.3 48.0 %all-to-all-start = ((bf16[64,36,128]{2,1,0:T(8,128)(2,1)}), bf16[64,36,128]{2,1,0:T(8,128)(2,1)S(1)}, u32[]{:S(2)}, u32[]{:S(2)}) async-start(bf16[64,36,128]{2,1,0:T(8,128)(2,1)} %convert_element_type.101), calls=%async_computation | async-start | bytes 1310720 | tf_op jit(solution)/shard_map/all_to_all | solution.py:44
  281.4 42.4 %all-to-all-start.1 = ((bf16[64,36,128]{2,1,0:T(8,128)(2,1)}), bf16[64,36,128]{2,1,0:T(8,128)(2,1)S(1)}, u32[]{:S(2)}, u32[]{:S(2)}) async-start(bf16[64,36,128]{2,1,0:T(8,128)(2,1)} %convert_element_type.104), calls=%async_computation.1 | async-start | bytes 1310720 | tf_op jit(solution)/shard_map/all_to_all | solution.py:44
  323.8 42.4 %all-to-all-start.2 = ((bf16[64,36,128]{2,1,0:T(8,128)(2,1)}), bf16[64,36,128]{2,1,0:T(8,128)(2,1)S(1)}, u32[]{:S(2)}, u32[]{:S(2)}) async-start(bf16[64,36,128]{2,1,0:T(8,128)(2,1)} %convert_element_type.107), calls=%async_computation.2 | async-start | bytes 1310720 | tf_op jit(solution)/shard_map/all_to_all | solution.py:44
  366.2 42.5 %all-to-all-start.3 = ((bf16[64,36,128]{2,1,0:T(8,128)(2,1)}), bf16[64,36,128]{2,1,0:T(8,128)(2,1)}, u32[]{:S(2)}, u32[]{:S(2)}) async-start(bf16[64,36,128]{2,1,0:T(8,128)(2,1)} %convert_element_type.110), calls=%async_computation.3 | async-start | bytes 1310720 | tf_op jit(solution)/shard_map/all_to_all | solution.py:44
  408.8 42.5 %all-to-all-start.4 = ((bf16[64,36,128]{2,1,0:T(8,128)(2,1)}), bf16[64,36,128]{2,1,0:T(8,128)(2,1)}, u32[]{:S(2)}, u32[]{:S(2)}) async-start(bf16[64,36,128]{2,1,0:T(8,128)(2,1)} %convert_element_type.113), calls=%async_computation.4 | async-start | bytes 1310720 | tf_op jit(solution)/shard_map/all_to_all | solution.py:44
  416.0 42.6 %copy-start.2 = (f32[1,36,1024]{2,0,1:T(1,128)S(1)}, f32[1,36,1024]{2,0,1:T(1,128)}, u32[]{:S(2)}) copy-start(f32[1,36,1024]{2,0,1:T(1,128)} %param.10) | copy-start | bytes 442372
  451.3 44.7 %all-to-all-start.5 = ((bf16[64,36,128]{2,1,0:T(8,128)(2,1)}), bf16[64,36,128]{2,1,0:T(8,128)(2,1)}, u32[]{:S(2)}, u32[]{:S(2)}) async-start(bf16[64,36,128]{2,1,0:T(8,128)(2,1)} %convert_element_type.116), calls=%async_computation.5 | async-start | bytes 1310720 | tf_op jit(solution)/shard_map/all_to_all | solution.py:44
  458.5 171.4 %all-gather.3.cloned.1.call-start = ((), (), s32[]{:S(2)}) async-start(), calls=%async_computation.8 | async-start | bytes 5324800 | tf_op jit(solution)/shard_map/all_gather | solution.py:54
  496.0 45.0 %all-to-all-start.6 = ((bf16[64,36,128]{2,1,0:T(8,128)(2,1)}), bf16[64,36,128]{2,1,0:T(8,128)(2,1)}, u32[]{:S(2)}, u32[]{:S(2)}) async-start(bf16[64,36,128]{2,1,0:T(8,128)(2,1)} %convert_element_type.119), calls=%async_computation.6 | async-start | bytes 1310720 | tf_op jit(solution)/shard_map/all_to_all | solution.py:44
  501.3 47.4 %copy-start.5 = (f32[1,36,128]{2,0,1:T(1,128)S(1)}, f32[1,36,128]{2,0,1:T(1,128)}, u32[]{:S(2)}) copy-start(f32[1,36,128]{2,0,1:T(1,128)} %param.12) | copy-start | bytes 55300
  541.1 86.0 %all-to-all-start.7 = ((bf16[64,36,128]{2,1,0:T(8,128)(2,1)}), bf16[64,36,128]{2,1,0:T(8,128)(2,1)}, u32[]{:S(2)}, u32[]{:S(2)}) async-start(bf16[64,36,128]{2,1,0:T(8,128)(2,1)} %convert_element_type.122), calls=%async_computation.7 | async-start | bytes 1310720 | tf_op jit(solution)/shard_map/all_to_all | solution.py:44
  622.2 6.3 copy-start.3
  622.2 6.3 copy-start.4
  637.2 4.7 copy-start.1
  637.2 4.7 copy-start.7
  1063.0 2.3 copy-start.6
Sparse Core Ops, SparseCore 0:
  462.1 161.4 all-gather.2
where the time goes:
time: 1080 us; the launch traced here: 1070 us
  blocking collectives  709 us (66%)
  waiting for transfers between devices  227 us (21%)
  starting transfers between devices  60.3 us (6%)
  matrix products  23.6 us (2%)
  local copies, waits for them, and re-layouts  23.1 us (2%)
  between operations  16.3 us (2%)
  other arithmetic  13.5 us (1%)
    unnamed x2, blocking collectives  637 us
    all_to_all x8, waiting for transfers between devices, weight_gradient(): lax.all_to_all(partial_sum.astype(jnp.bfloat16), 'fsdp', split_axis=0, co...  227 us
    psum x1, blocking collectives, synchronise(): summed = lax.psum(snapshot[0], 'group')  72.4 us
    all_to_all x8, starting transfers between devices, weight_gradient(): lax.all_to_all(partial_sum.astype(jnp.bfloat16), 'fsdp', split_axis=0, co...  60.3 us
  transfers between devices with their start and end apart: 9, of which 7 were waited for; matrix products, arithmetic and copies ran while one was open for 3% of the time, Pallas kernels for 0%

commit v1 on v0

v1 whole, which is shorter than its diff:
```python
import functools

import jax
import jax.numpy as jnp
from jax import lax
from jax.experimental import pallas as pl
from jax.experimental.pallas import tpu as pltpu
from jax.sharding import PartitionSpec as P

MESH = pl.DeviceIdType.MESH
F32 = jnp.float32
BF16 = jnp.bfloat16

D = 2304
KV = 1024
FW = 128
FRAGS = 8
TOK = 256
NZ = 8
NY = 4
NE = 8
NX = 4
ROWS = 36
CHIP = 72
SLAB = 288
HALF = 512

epsilon = 1e-06
inner_rate = 0.05
gain_rate = 0.002
momentum = 0.9
outer_rate = 0.7
mixing = 0.5
FACTOR = D ** (-0.5)


def window_start(z):
    return (SLAB * z) // 128


def order(z, s):
    near = jnp.where(z > 3, 7 - z, z)
    first = 7 - 2 * near
    k = s - first
    two_sided = jnp.where(k % 2 == 0, 2 * near - k // 2, (k - 1) // 2)
    slab = jnp.where(s < first, 7 - s, two_sided)
    slab = jnp.where(z > 3, 7 - slab, slab)
    return jnp.where(s == 7, z, slab)


def step_kernel(
    frag_ref, hid_hbm, gv_hbm, w_ref, gains_ref, snap_ref, outer_ref, mom_ref,
    values_hbm, gh_hbm, neww_ref, ggrad_ref, newo_ref, newm_ref,
    hid, gx, nbx, wp, w, stage, pack, dw, s1, r1, s2, r2, racc, sz, rz, fbuf,
    ig, vout, gh, invb, grow, gacc, g1, g2, hsrc, h1, h2, sx, szh,
    in_sem, out_sem, agz_s, agz_r, ay_s, ay_r, tw_s, tw_r, nx_s, nx_r,
    ry_s, ry_r, rz_s, rz_r, f_s, f_r,
    g1_s, g1_r, g2_s, g2_r, h1_s, h1_r, h2_s, h2_r, sx_s, sx_r, szh_s, szh_r,
):
    g = lax.axis_index("group")
    f = lax.axis_index("fsdp")
    x, zh = g // 2, g % 2
    z, e = f // NE, f % NE
    y, c = e // 2, e % 2
    yr, yl, yo = (y + 1) % NY, (y + 3) % NY, (y + 2) % NY
    twin = (g, f + 1 - 2 * c)

    def at(zz, yy):
        return (g, zz * NE + yy * 2 + c)

    right, left = at(z, yr), at(z, yl)
    up, down = at(z + 1, y), at(z - 1, y)
    e_peers = [((e + k) % NE, (g, z * NE + (e + k) % NE)) for k in range(1, NE)]
    z_peers = [((z + k) % NZ, (g, ((z + k) % NZ) * NE + e)) for k in range(1, NZ)]
    x_peers = [((x + k) % NX, (((x + k) % NX) * 2 + zh, f)) for k in range(1, NX)]
    zh_peer = (x * 2 + 1 - zh, f)

    def remote(src, dst, send, recv, device):
        return pltpu.make_async_remote_copy(
            src_ref=src, dst_ref=dst, send_sem=send, recv_sem=recv, device_id=device, device_id_type=MESH
        )

    hid_in = pltpu.make_async_copy(hid_hbm, hid, in_sem.at[0])
    gv_in = pltpu.make_async_copy(gv_hbm, gx.at[c], in_sem.at[1])
    hid_in.start()
    gv_in.start()

    barrier = pltpu.get_barrier_semaphore()
    peers = [p for _, p in e_peers] + [p for _, p in z_peers] + [p for _, p in x_peers] + [zh_peer]
    for peer in peers:
        pl.semaphore_signal(barrier, inc=1, device_id=peer, device_id_type=MESH)

    for h in range(2):
        for q in range(4):
            pack[h, ROWS * q : ROWS * (q + 1), :] = w_ref[0, :, HALF * h + 128 * q : HALF * h + 128 * (q + 1)]
    wp[c, z, y] = pack[...].astype(BF16)

    gain_own = jnp.broadcast_to(gains_ref[...].astype(BF16), (8, ROWS))
    first_lane = ROWS * f - 128 * window_start(z)
    spot = lax.broadcasted_iota(jnp.int32, (ROWS, 128), 0) + first_lane
    lane = lax.broadcasted_iota(jnp.int32, (ROWS, 128), 1)
    g1[e] = jnp.zeros((8, 128), F32)
    for r in range(3):
        hot = jnp.where(spot == lane + 128 * r, 1.0, 0.0).astype(BF16)
        g1[e, r : r + 1, :] = jnp.dot(gain_own, hot, preferred_element_type=F32)[0:1]
    sx[x] = jnp.zeros((40, 128), F32)
    sx[x, 0:ROWS, :] = snap_ref[0]

    pl.semaphore_wait(barrier, len(peers))

    def spread_start(buf, own, peer_list, send, recv, src=None):
        for index, peer in peer_list:
            source = buf.at[own] if src is None else src.at[index]
            remote(source, buf.at[own], send.at[index], recv.at[own], peer).start()

    def spread_wait(buf, own, peer_list, send, recv):
        for index, peer in peer_list:
            remote(buf.at[index], buf.at[index], send.at[index], recv.at[index], peer).wait_recv()

    def spread_done(buf, own, peer_list, send, recv, src=None):
        for index, peer in peer_list:
            source = buf.at[own] if src is None else src.at[index]
            remote(source, buf.at[own], send.at[index], recv.at[own], peer).wait_send()

    def total(buf, count):
        result = buf[0]
        for index in range(1, count):
            result = result + buf[index]
        return result

    def z_copy(direction, slab):
        return remote(
            wp.at[c, slab, y], wp.at[c, slab, y], agz_s.at[direction, slab], agz_r.at[direction, slab],
            up if direction == 0 else down,
        )

    def y_copy(kind, slab):
        device = right if kind in (0, 2) else left
        if kind < 2:
            ref = wp.at[c, slab, y]
        elif kind == 2:
            ref = wp.at[c, slab, yl, 0]
        else:
            ref = wp.at[c, slab, yr, 1]
        return remote(ref, ref, ay_s.at[kind, slab], ay_r.at[kind, slab], device)

    def y_arrival(kind, slab):
        ref = [wp.at[c, slab, yl], wp.at[c, slab, yr], wp.at[c, slab, yo, 0], wp.at[c, slab, yo, 1]][kind]
        return remote(ref, ref, ay_s.at[kind, slab], ay_r.at[kind, slab], right)

    def twin_copy(slab, core):
        return remote(wp.at[core, slab], wp.at[core, slab], tw_s.at[slab], tw_r.at[slab], twin)

    def gather_z(t):
        if t == 0:
            @pl.when(z < NZ - 1)
            def _():
                z_copy(0, z).start()

            @pl.when(z > 0)
            def _():
                z_copy(1, z).start()

            y_copy(0, z).start()
            y_copy(1, z).start()
            return

        @pl.when(z - t >= 0)
        def _():
            slab = z - t
            z_copy(0, slab).wait_recv()

            @pl.when(z < NZ - 1)
            def _():
                z_copy(0, slab).start()

            y_copy(0, slab).start()
            y_copy(1, slab).start()

        @pl.when(z + t <= NZ - 1)
        def _():
            slab = z + t
            z_copy(1, slab).wait_recv()

            @pl.when(z > 0)
            def _():
                z_copy(1, slab).start()

            y_copy(0, slab).start()
            y_copy(1, slab).start()

    def gather_y(j):
        slab = order(z, 7 - j)
        y_arrival(0, slab).wait_recv()
        y_copy(2, slab).start()
        y_arrival(1, slab).wait_recv()
        y_copy(3, slab).start()

    def gather_twin(j):
        slab = order(z, 7 - j)
        y_arrival(2, slab).wait_recv()
        y_arrival(3, slab).wait_recv()
        twin_copy(slab, c).start()

    def unpack(lo, hi):
        def one(j, _):
            slab = order(z, 7 - j)
            twin_copy(slab, 1 - c).wait_recv()
            for core in range(2):
                for yy in range(NY):
                    for h in range(2):
                        block = wp[core, slab, yy, h].astype(F32)
                        base = ROWS * (2 * yy + core)
                        for q in range(4):
                            stage[base : base + ROWS, HALF * h + 128 * q : HALF * h + 128 * (q + 1)] = block[
                                ROWS * q : ROWS * (q + 1)
                            ]
            w[pl.ds(pl.multiple_of(SLAB * slab, 16), SLAB), :] = stage[...].astype(BF16)
            return 0

        lax.fori_loop(lo, hi, one, 0)

    def norms():
        def one(r, _):
            rows = pl.ds(pl.multiple_of(32 * r, 32), 32)
            tokens = hid[rows, :].astype(F32)
            mean = jnp.sum(tokens * tokens, axis=-1, keepdims=True) / D
            invb[rows, :] = jnp.broadcast_to(lax.rsqrt(mean + epsilon), (32, 128))
            return 0

        lax.fori_loop(0, TOK // 32, one, 0)

    def normalise():
        def one(r, _):
            rows = pl.ds(pl.multiple_of(32 * r, 32), 32)
            normed = hid[rows, :].astype(F32) * invb[rows, 0:1]
            nbx[c, rows, :] = (normed * grow[0:1, :]).astype(BF16)
            return 0

        lax.fori_loop(0, TOK // 32, one, 0)

    nx_nb = lambda core: remote(nbx.at[core], nbx.at[core], nx_s.at[0], nx_r.at[0], twin)
    nx_gv = lambda core: remote(gx.at[core], gx.at[core], nx_s.at[1], nx_r.at[1], twin)

    def weight_terms():
        columns = pl.ds(pl.multiple_of(HALF * c, 128), HALF)

        def one(k, _):
            feats = pl.ds(pl.multiple_of(256 * k, 256), 256)
            dims = (((0,), (0,)), ((), ()))
            dw[feats, :] = lax.dot_general(
                nbx[0, :, feats], gx[0, :, columns], dims, preferred_element_type=F32
            ) + lax.dot_general(nbx[1, :, feats], gx[1, :, columns], dims, preferred_element_type=F32)
            return 0

        lax.fori_loop(0, D // 256, one, 0)

    def term(slab, yy, h):
        rows = pl.ds(pl.multiple_of(CHIP * (NY * slab + yy), 8), CHIP)
        return jnp.concatenate([dw[rows, 256 * h : 256 * h + 128], dw[rows, 256 * h + 128 : 256 * h + 256]], axis=0)

    def far_copy(kind, slab):
        return remote(
            s1.at[slab, kind], r1.at[slab, kind], ry_s.at[kind, slab], ry_r.at[kind, slab], right if kind == 0 else left
        )

    def near_copy(kind, slab):
        return remote(
            s2.at[slab, kind], r2.at[slab, kind], ry_s.at[2 + kind, slab], ry_r.at[2 + kind, slab],
            right if kind == 0 else left,
        )

    def chain_copy(direction, slab):
        return remote(
            sz.at[slab], rz.at[direction, slab], rz_s.at[direction, slab], rz_r.at[direction, slab],
            up if direction == 0 else down,
        )

    def reduce_far(s):
        slab = order(z, s)
        for h in range(2):
            s1[slab, h] = term(slab, yo, h).astype(BF16)
            far_copy(h, slab).start()

    def reduce_near(s):
        slab = order(z, s)
        for kind, yy in ((0, yr), (1, yl)):
            far_copy(kind, slab).wait_recv()
            s2[slab, kind, kind] = (term(slab, yy, kind) + r1[slab, kind].astype(F32)).astype(BF16)
            s2[slab, kind, 1 - kind] = term(slab, yy, 1 - kind).astype(BF16)
            near_copy(kind, slab).start()

    def reduce_row(s):
        slab = order(z, s)
        near_copy(0, slab).wait_recv()
        near_copy(1, slab).wait_recv()
        for h in range(2):
            racc[slab, h] = term(slab, y, h) + r2[slab, 0, h].astype(F32) + r2[slab, 1, h].astype(F32)

    def reduce_chain(u):
        if u == NZ - 1:
            @pl.when(z > 0)
            def _():
                chain_copy(0, z).wait_recv()
                racc[z] = racc[z] + rz[0, z].astype(F32)

            @pl.when(z < NZ - 1)
            def _():
                chain_copy(1, z).wait_recv()
                racc[z] = racc[z] + rz[1, z].astype(F32)

            return

        @pl.when(z <= u)
        def _():
            slab = NZ - 1 + z - u

            @pl.when(z > 0)
            def _():
                chain_copy(0, slab).wait_recv()
                sz[slab] = (racc[slab] + rz[0, slab].astype(F32)).astype(BF16)

            @pl.when(z == 0)
            def _():
                sz[slab] = racc[slab].astype(BF16)

            chain_copy(0, slab).start()

        @pl.when(z >= NZ - 1 - u)
        def _():
            slab = z - (NZ - 1) + u

            @pl.when(z < NZ - 1)
            def _():
                chain_copy(1, slab).wait_recv()
                sz[slab] = (racc[slab] + rz[1, slab].astype(F32)).astype(BF16)

            @pl.when(z == NZ - 1)
            def _():
                sz[slab] = racc[slab].astype(BF16)

            chain_copy(1, slab).start()

    def make_values():
        def one(n, _):
            columns = pl.ds(pl.multiple_of(256 * n, 256), 256)
            vout[:, columns] = (jnp.dot(nbx[c], w[:, columns], preferred_element_type=F32) * FACTOR).astype(BF16)
            return 0

        lax.fori_loop(0, KV // 256, one, 0)

    values_out = pltpu.make_async_copy(vout, values_hbm, out_sem.at[0])
    gh_out = pltpu.make_async_copy(gh, gh_hbm, out_sem.at[1])

    def input_gradient(lo, hi):
        def one(k, _):
            feats = pl.ds(pl.multiple_of(256 * k, 256), 256)
            ig[:, feats] = (
                lax.dot_general(gx[c], w[feats, :], (((1,), (1,)), ((), ())), preferred_element_type=F32) * FACTOR
            )
            return 0

        lax.fori_loop(lo, hi, one, 0)

    def hidden_gradient(lo, hi):
        def one(r, _):
            rows = pl.ds(pl.multiple_of(32 * r, 32), 32)
            inverse = invb[rows, 0:1]
            normed = hid[rows, :].astype(F32) * inverse
            grad = ig[rows, :]
            along = grad * normed
            gacc[...] += jnp.sum(along.reshape(4, 8, D), axis=0)
            gain = grow[0:1, :]
            mean = jnp.sum(along * gain, axis=-1, keepdims=True) / D
            gh[rows, :] = (inverse * (grad * gain - normed * mean)).astype(BF16)
            return 0

        lax.fori_loop(lo, hi, one, 0)

    gather_z(0)
    spread_start(g1, e, e_peers, g1_s, g1_r)
    spread_start(sx, x, x_peers, sx_s, sx_r)
    gv_in.wait()
    nx_gv(c).start()
    hid_in.wait()
    norms()
    spread_wait(g1, e, e_peers, g1_s, g1_r)
    g2[z] = total(g1, NE)
    spread_start(g2, z, z_peers, g2_s, g2_r)
    gather_z(1)
    gather_z(2)
    gather_y(0)
    spread_wait(g2, z, z_peers, g2_s, g2_r)
    grow[...] = jnp.zeros((8, D), F32)
    for slab in range(NZ):
        for r in range(3):
            lanes = slice(128 * (window_start(slab) + r), 128 * (window_start(slab) + r + 1))
            grow[0:1, lanes] = grow[0:1, lanes] + g2[slab, r : r + 1, :]
    normalise()
    nx_nb(c).start()
    spread_wait(sx, x, x_peers, sx_s, sx_r)
    szh[zh] = total(sx, NX)
    szh_copy = remote(szh.at[zh], szh.at[zh], szh_s, szh_r, zh_peer)
    szh_copy.start()
    gather_z(3)
    gather_y(1)
    gather_twin(0)
    nx_gv(1 - c).wait_recv()
    nx_nb(1 - c).wait_recv()
    weight_terms()
    reduce_far(0)
    reduce_far(1)
    reduce_far(2)
    gather_z(4)
    gather_y(2)
    gather_twin(1)
    gather_z(5)
    gather_y(3)
    gather_twin(2)
    reduce_near(0)
    reduce_far(3)
    gather_z(6)
    gather_y(4)
    gather_twin(3)
    reduce_near(1)
    reduce_far(4)
    gather_z(7)
    gather_y(5)
    gather_twin(4)
    reduce_row(0)
    reduce_chain(0)
    reduce_near(2)
    reduce_far(5)
    gather_y(6)
    gather_twin(5)
    reduce_row(1)
    reduce_chain(1)
    reduce_near(3)
    reduce_far(6)
    gather_y(7)
    gather_twin(6)
    unpack(0, 4)
    reduce_row(2)
    reduce_chain(2)
    reduce_near(4)
    reduce_far(7)
    gather_twin(7)
    reduce_row(3)
    reduce_chain(3)
    reduce_near(5)
    unpack(4, 8)
    reduce_row(4)
    reduce_chain(4)
    reduce_near(6)
    make_values()
    values_out.start()
    reduce_row(5)
    reduce_chain(5)
    reduce_near(7)
    input_gradient(0, 9)
    reduce_row(6)
    reduce_chain(6)
    gacc[...] = jnp.zeros((8, D), F32)
    hidden_gradient(0, 8)
    gh_out.start()
    gain_row = jnp.sum(gacc[...], axis=0, keepdims=True)
    hsrc[...] = jnp.zeros((NZ, 8, 128), F32)
    for slab in range(NZ):
        for r in range(3):
            lanes = slice(128 * (window_start(slab) + r), 128 * (window_start(slab) + r + 1))
            hsrc[slab, r : r + 1, :] = gain_row[:, lanes]
    h1[z] = hsrc[z]
    spread_start(h1, z, z_peers, h1_s, h1_r, src=hsrc)
    reduce_row(7)
    reduce_chain(7)
    fbuf[c] = racc[z]
    last = lambda core: remote(fbuf.at[core], fbuf.at[core], f_s, f_r, twin)
    last(c).start()
    spread_wait(h1, z, z_peers, h1_s, h1_r)
    h2[e] = total(h1, NZ)
    spread_start(h2, e, e_peers, h2_s, h2_r)

    remote(szh.at[1 - zh], szh.at[1 - zh], szh_s, szh_r, zh_peer).wait_recv()
    change = outer_ref[...] - (szh[0] + szh[1])[0:ROWS] / (2 * NX)
    new_moment = momentum * mom_ref[...] + change
    new_outer = outer_ref[...] - outer_rate * (change + momentum * new_moment)
    newm_ref[...] = new_moment
    newo_ref[...] = new_outer

    last(1 - c).wait_recv()
    for core in range(2):
        @pl.when(c == core)
        def _():
            for j in range(FRAGS):
                q = j % 4
                base = CHIP * (q % 2) + ROWS * core
                grad = fbuf[j // 4, q // 2, base : base + ROWS, :] * FACTOR
                inner = w_ref[0, :, 128 * j : 128 * (j + 1)] - inner_rate * grad
                mixed = mixing * inner + (1.0 - mixing) * newo_ref[...]
                neww_ref[0, :, 128 * j : 128 * (j + 1)] = jnp.where(frag_ref[0] == j, mixed, inner)

    spread_wait(h2, e, e_peers, h2_s, h2_r)
    ggrad_ref[...] = total(h2, NE)

    values_out.wait()
    gh_out.wait()
    for t in range(NZ):
        @pl.when(jnp.logical_and(z - t >= 0, z < NZ - 1))
        def _():
            z_copy(0, z - t).wait_send()

        @pl.when(jnp.logical_and(z + t <= NZ - 1, z > 0))
        def _():
            z_copy(1, z + t).wait_send()

    def drain(slab, _):
        for kind in range(4):
            y_copy(kind, slab).wait_send()
        twin_copy(slab, c).wait_send()
        for kind in range(2):
            far_copy(kind, slab).wait_send()
            near_copy(kind, slab).wait_send()

        @pl.when(slab > z)
        def _():
            chain_copy(0, slab).wait_send()

        @pl.when(slab < z)
        def _():
            chain_copy(1, slab).wait_send()

        return 0

    lax.fori_loop(0, NZ, drain, 0)
    nx_nb(c).wait_send()
    nx_gv(c).wait_send()
    last(c).wait_send()
    szh_copy.wait_send()
    spread_done(g1, e, e_peers, g1_s, g1_r)
    spread_done(g2, z, z_peers, g2_s, g2_r)
    spread_done(h1, z, z_peers, h1_s, h1_r, src=hsrc)
    spread_done(h2, e, e_peers, h2_s, h2_r)
    spread_done(sx, x, x_peers, sx_s, sx_r)


def body(hidden, grad_values, weights, gains, snapshot, outer_frag, outer_moment, fragment_index):
    vmem = pl.BlockSpec(memory_space=pltpu.VMEM)
    anywhere = pl.BlockSpec(memory_space=pl.ANY)
    dma = pltpu.SemaphoreType.DMA
    values, grad_hidden, new_weights, gain_window, new_outer, new_moment = pl.pallas_call(
        step_kernel,
        out_shape=(
            jax.ShapeDtypeStruct((TOK, KV), BF16),
            jax.ShapeDtypeStruct((TOK, D), BF16),
            jax.ShapeDtypeStruct((1, ROWS, KV), F32),
            jax.ShapeDtypeStruct((8, 128), F32),
            jax.ShapeDtypeStruct((ROWS, FW), F32),
            jax.ShapeDtypeStruct((ROWS, FW), F32),
        ),
        in_specs=[pl.BlockSpec(memory_space=pltpu.SMEM), anywhere, anywhere, vmem, vmem, vmem, vmem, vmem],
        out_specs=(anywhere, anywhere, vmem, vmem, vmem, vmem),
        scratch_shapes=[
            pltpu.VMEM((TOK, D), BF16),
            pltpu.VMEM((2, TOK, KV), BF16),
            pltpu.VMEM((2, TOK, D), BF16),
            pltpu.VMEM((2, NZ, NY, 2, 144, 128), BF16),
            pltpu.VMEM((D, KV), BF16),
            pltpu.VMEM((SLAB, KV), F32),
            pltpu.VMEM((2, 144, 128), F32),
            pltpu.VMEM((D, HALF), F32),
            pltpu.VMEM((NZ, 2, 144, 128), BF16),
            pltpu.VMEM((NZ, 2, 144, 128), BF16),
            pltpu.VMEM((NZ, 2, 2, 144, 128), BF16),
            pltpu.VMEM((NZ, 2, 2, 144, 128), BF16),
            pltpu.VMEM((NZ, 2, 144, 128), F32),
            pltpu.VMEM((NZ, 2, 144, 128), BF16),
            pltpu.VMEM((2, NZ, 2, 144, 128), BF16),
            pltpu.VMEM((2, 2, 144, 128), F32),
            pltpu.VMEM((TOK, D), F32),
            pltpu.VMEM((TOK, KV), BF16),
            pltpu.VMEM((TOK, D), BF16),
            pltpu.VMEM((TOK, 128), F32),
            pltpu.VMEM((8, D), F32),
            pltpu.VMEM((8, D), F32),
            pltpu.VMEM((NE, 8, 128), F32),
            pltpu.VMEM((NZ, 8, 128), F32),
            pltpu.VMEM((NZ, 8, 128), F32),
            pltpu.VMEM((NZ, 8, 128), F32),
            pltpu.VMEM((NE, 8, 128), F32),
            pltpu.VMEM((NX, 40, 128), F32),
            pltpu.VMEM((2, 40, 128), F32),
            dma((2,)), dma((2,)),
            dma((2, NZ)), dma((2, NZ)),
            dma((4, NZ)), dma((4, NZ)),
            dma((NZ,)), dma((NZ,)),
            dma((2,)), dma((2,)),
            dma((4, NZ)), dma((4, NZ)),
            dma((2, NZ)), dma((2, NZ)),
            dma, dma,
            dma((NE,)), dma((NE,)),
            dma((NZ,)), dma((NZ,)),
            dma((NZ,)), dma((NZ,)),
            dma((NE,)), dma((NE,)),
            dma((NX,)), dma((NX,)),
            dma, dma,
        ],
        compiler_params=pltpu.CompilerParams(
            collective_id=0, has_side_effects=True, vmem_limit_bytes=56 * 1024 * 1024
        ),
        cost_estimate=pl.CostEstimate(flops=3 * 2 * TOK * D * KV, bytes_accessed=4_000_000, transcendentals=0),
    )(fragment_index, hidden, grad_values, weights, gains, snapshot, outer_frag, outer_moment)
    f = lax.axis_index("fsdp")
    offset = ROWS * f - 128 * window_start(f // NE)
    gain_grad = lax.dynamic_slice_in_dim(gain_window.reshape(-1), offset, ROWS, 0)
    new_gains = gains - gain_rate * gain_grad[None]
    return (values, grad_hidden, new_weights, new_gains, new_outer, new_moment)


def solution(mesh):
    return jax.shard_map(
        body,
        mesh=mesh,
        in_specs=(
            P(("group", "fsdp"), None),
            P(("group", "fsdp"), None),
            P("group", "fsdp", None),
            P("group", "fsdp"),
            P("group", "fsdp", None),
            P("fsdp", None),
            P("fsdp", None),
            P(),
        ),
        out_specs=(
            P(("group", "fsdp"), None),
            P(("group", "fsdp"), None),
            P("group", "fsdp", None),
            P("group", "fsdp"),
            P("fsdp", None),
            P("fsdp", None),
        ),
        check_vma=False,
    )
```

time: 1080 us -> 99.5 us (0.09)
  blocking collectives: 709 us -> 0 us
  waiting for transfers between devices: 227 us -> 0 us
  Pallas kernels: 0 us -> 87.7 us
  starting transfers between devices: 60.3 us -> 0 us
  matrix products: 23.6 us -> 0 us
  between operations: 16.3 us -> 1.35 us
  local copies, waits for them, and re-layouts: 23.1 us -> 8.77 us
  other arithmetic: 13.5 us -> 1.36 us
    unnamed x2 -> x0, blocking collectives: 637 us -> none
    all_to_all x8 -> x0, waiting for transfers between devices: 227 us -> none  [weight_gradient(): lax.all_to_all(partial_sum.astype(jnp.bfloat16), 'fsdp', split_axis=0, co...]
    pallas_call x0 -> x1, Pallas kernels: none -> 87.7 us  [body(): pl.pallas_call(step_kernel, out_shape=(jax.ShapeDtypeStruct((TOK, KV), BF...]
    psum x1 -> x0, blocking collectives: 72.4 us -> none  [synchronise(): summed = lax.psum(snapshot[0], 'group')]
    all_to_all x8 -> x0, starting transfers between devices: 60.3 us -> none  [weight_gradient(): lax.all_to_all(partial_sum.astype(jnp.bfloat16), 'fsdp', split_axis=0, co...]
    dot_general x10 -> x0, matrix products: 23.6 us -> none  [the longest x8 16.5 us: weight_gradient(): lax.dot_general(normed_bf, cotangent, (((0,), (0,)), ((), ())), preferred...]
    convert_element_type x8 -> x0, local copies, waits for them, and re-layouts: 12.7 us -> none  [weight_gradient(): partial_sum.astype(jnp.bfloat16)]
  transfers between devices with their start and end apart: 9 -> 0, of which waited for: 7 -> 0; matrix products, arithmetic and copies ran while one was open for 3% -> 0% of each run, Pallas kernels for 0% -> 0%
where the time goes in v1:
time: 99.5 us; the launch traced here: 99.2 us
  Pallas kernels  87.7 us (88%)
  local copies, waits for them, and re-layouts  8.77 us (9%)
  other arithmetic  1.36 us (1%)
  between operations  1.35 us (1%)
    pallas_call x1, Pallas kernels, body(): pl.pallas_call(step_kernel, out_shape=(jax.ShapeDtypeStruct((TOK, KV), BF...  87.7 us
    unnamed x15, local copies, waits for them, and re-layouts  8.77 us

profile of v1, /device:TPU:1, one launch (start us, length us, event | category | flops | bytes accessed | tf_op | source)
XLA Modules:
  0.0 99.2 jit_solution(1221111999508690743)
XLA Ops:
  1.3 1.3 %copy.15.snap_ref = f32[1,36,128]{2,1,0:T(8,128)} copy(f32[1,36,128]{2,0,1:T(1,128)} %param.12) | data formatting | bytes 36864 | tf_op args[4]
  2.7 1.6 %copy.14.w_ref = f32[1,36,1024]{2,1,0:T(8,128)} copy(f32[1,36,1024]{2,0,1:T(1,128)} %param.10) | data formatting | bytes 294912 | tf_op args[2]
  4.3 0.0 copy-start.3
  4.3 87.7 %shard_map.127 = (bf16[256,1024]{1,0:T(8,128)(2,1)}, bf16[256,2304]{1,0:T(8,128)(2,1)}, f32[1,36,1024]{2,1,0:T(8,128)}, f32[8,128]{1,0:T(8,128)}, f32[36,128]{1,0:T(8,128)}, /*index=5*/f32[36,128]{1,0:T(8,128)}) custom-call(s32[1]{0:T(128)S(6)} %copy.21.frag_ref, bf16[256,2304]{1,0:T(8,128)(2,1)} %hid_hbm.1, bf16[256,1024]{1,0:T(8,128)(2,1)} %gv_hbm.1, ...), custom_call_target="tpu_custom_call" | custom-call | flops 3623878656 | bytes 4000000 | tf_op jit(solution)/shard_map/pallas_call | solution.py:550
  92.0 0.0 copy-start
  92.0 0.0 copy-done.3
  92.0 1.4 %bitcast_subtract_fusion = f32[1,36]{1,0:T(1,128)} fusion(f32[1,36]{1,0:T(1,128)S(1)} %copy-done.3, f32[1024]{0:T(1024)} %bitcast.3, s32[]{:T(128)S(6)} %select_n.13), kind=kLoop, calls=%fused_computation | loop fusion | flops 72 | bytes 436 | tf_op jit(solution)/shard_map/sub | solution.py:615
  93.4 1.7 %copy.16 = f32[1,36,1024]{2,0,1:T(1,128)} copy(f32[1,36,1024]{2,1,0:T(8,128)} %get-tuple-element.20) | data formatting | bytes 294912
  95.1 1.9 %copy.22 = bf16[256,1024]{1,0:T(8,128)(2,1)} copy(bf16[256,1024]{1,0:T(8,128)(2,1)} %get-tuple-element.30) | data formatting | bytes 1048576
  97.0 0.0 copy-done
  97.0 0.0 copy-start.2
  97.0 0.0 copy-start.1
  97.0 1.0 %copy.23 = bf16[256,2304]{1,0:T(8,128)(2,1)} copy(bf16[256,2304]{1,0:T(8,128)(2,1)S(1)} %copy-done) | data formatting | bytes 2359296
  98.0 0.0 copy-done.2
  98.0 0.6 copy.24
  98.6 0.0 copy-done.1
  98.6 0.6 copy.25
Async XLA Ops:
  4.3 87.7 %copy-start.3 = (f32[1,36]{1,0:T(1,128)S(1)}, f32[1,36]{1,0:T(1,128)}, u32[]{:S(2)}) copy-start(f32[1,36]{1,0:T(1,128)} %gains_ref.1) | copy-start | bytes 436
  92.0 5.0 %copy-start = (bf16[256,2304]{1,0:T(8,128)(2,1)S(1)}, bf16[256,2304]{1,0:T(8,128)(2,1)}, u32[]{:S(2)}) copy-start(bf16[256,2304]{1,0:T(8,128)(2,1)} %get-tuple-element.31) | copy-start | bytes 3538948
  97.0 1.0 %copy-start.2 = (f32[36,128]{1,0:T(8,128)S(1)}, f32[36,128]{1,0:T(8,128)}, u32[]{:S(2)}) copy-start(f32[36,128]{1,0:T(8,128)} %get-tuple-element.34) | copy-start | bytes 55300
  97.0 1.6 %copy-start.1 = (f32[36,128]{1,0:T(8,128)S(1)}, f32[36,128]{1,0:T(8,128)}, u32[]{:S(2)}) copy-start(f32[36,128]{1,0:T(8,128)} %get-tuple-element.35) | copy-start | bytes 55300

commit v2 on v0

v2 whole, which is shorter than its diff:
```python
import functools

import jax
import jax.numpy as jnp
from jax import lax
from jax.experimental import pallas as pl
from jax.experimental.pallas import tpu as pltpu
from jax.sharding import PartitionSpec as P

MESH = pl.DeviceIdType.MESH
F32 = jnp.float32
BF16 = jnp.bfloat16

D = 2304
KV = 1024
FW = 128
FRAGS = 8
TOK = 256
NZ = 8
NY = 4
NE = 8
NX = 4
ROWS = 36
CHIP = 72
SLAB = 288
HALF = 512

epsilon = 1e-06
inner_rate = 0.05
gain_rate = 0.002
momentum = 0.9
outer_rate = 0.7
mixing = 0.5
FACTOR = D ** (-0.5)
BLOCK = 288
ZH = 112
VR = 64
VH = VR // 2


def window_start(z):
    return (SLAB * z) // 128


def order(z, s):
    pair, odd = z // 2, z % 2
    near = 3 - s // 2
    low = jnp.where(pair % 3 == 0, near, jnp.where(near < 2, 1 - near, near))
    which = jnp.where(pair > 1, 3 - low, low)
    return 2 * which + jnp.where(s % 2 == 0, 1 - odd, odd)


def step_kernel(
    frag_ref, hid_hbm, gv_hbm, w_hbm, gains_hbm, snap_hbm, outer_hbm, mom_hbm,
    values_hbm, gh_hbm, neww_hbm, newg_hbm, newo_hbm, newm_hbm,
    hid, gx, nbx, nbg, wp, w, stage, pack, dw, s1, r1, s2, r2, racc, sp, rp, sz, rz,
    vacc, vs1, vr1, vs2, vr2, vz, rv, fbuf,
    ig, vout, gh, invb, grow, gacc, g0, g1, g2, hsrc, h1, h2, sx, szh,
    w_ref, gains_ref, snap_ref, outer_ref, mom_ref, neww_ref, newg_ref, newo_ref, newm_ref,
    in_sem, out_sem, agz_s, agz_r, agp_s, agp_r, agv_s, agv_r, ay_s, ay_r, av_s, av_r, tw_s, tw_r, nx_s, nx_r,
    ry_s, ry_r, rp_s, rp_r, rz_s, rz_r, rv_s, rv_r, vy_s, vy_r, f_s, f_r,
    g0_s, g0_r, g1_s, g1_r, g2_s, g2_r, h1_s, h1_r, h2_s, h2_r, sx_s, sx_r, szh_s, szh_r, token,
):
    g = lax.axis_index("group")
    f = lax.axis_index("fsdp")
    x, zh = g // 2, g % 2
    z, e = f // NE, f % NE
    y, c = e // 2, e % 2
    yr, yl, yo = (y + 1) % NY, (y + 3) % NY, (y + 2) % NY
    twin = (g, f + 1 - 2 * c)

    def at(zz, yy):
        return (g, zz * NE + yy * 2 + c)

    right, left = at(z, yr), at(z, yl)
    up, down = at(z + 1, y), at(z - 1, y)
    mate, up_two, down_two = at(z + 1 - 2 * (z % 2), y), at(z + 2, y), at(z - 2, y)
    pair, z_mate = z // 2, z + 1 - 2 * (z % 2)
    pairs = NZ // 2
    e_peers = [((e + k) % NE, (g, z * NE + (e + k) % NE)) for k in range(1, NE)]
    z_peers = [((z + k) % NZ, (g, ((z + k) % NZ) * NE + e)) for k in range(1, NZ)]
    xr, xl, xo = (x + 1) % NX, (x + 3) % NX, (x + 2) % NX
    x_right, x_left = (xr * 2 + zh, f), (xl * 2 + zh, f)
    after = (x * 2 + (zh + (z + 1) // NZ) % 2, ((z + 1) % NZ) * NE + e)
    before = (x * 2 + (zh + (NZ - z) // NZ) % 2, ((z + NZ - 1) % NZ) * NE + e)
    zh_peer = (x * 2 + 1 - zh, f)

    def remote(src, dst, send, recv, device):
        return pltpu.make_async_remote_copy(
            src_ref=src, dst_ref=dst, send_sem=send, recv_sem=recv, device_id=device, device_id_type=MESH
        )

    barrier = pltpu.get_barrier_semaphore()
    peers = [before, after, right, left, x_right, x_left, twin]
    two_after, two_before = at((z + 2) % NZ, y), at((z + NZ - 2) % NZ, y)
    peers += [two_after, two_before]
    for peer in peers:
        pl.semaphore_signal(barrier, inc=1, device_id=peer, device_id_type=MESH)

    w_in = pltpu.make_async_copy(w_hbm, w_ref, in_sem.at[0])
    gains_in = pltpu.make_async_copy(gains_hbm, gains_ref, in_sem.at[1])
    snap_in = pltpu.make_async_copy(snap_hbm, snap_ref, in_sem.at[2])
    hid_in = pltpu.make_async_copy(hid_hbm, hid, in_sem.at[3])
    gv_in = pltpu.make_async_copy(gv_hbm, gx.at[c], in_sem.at[4])
    outer_in = pltpu.make_async_copy(outer_hbm, outer_ref, in_sem.at[5])
    mom_in = pltpu.make_async_copy(mom_hbm, mom_ref, in_sem.at[6])
    for copy in (gains_in, w_in, hid_in, gv_in, snap_in, outer_in, mom_in):
        copy.start()

    def own_columns(j):
        return pl.ds(j, ROWS, stride=FRAGS)

    def pack_own():
        w_in.wait()
        for q in range(FRAGS):
            pack[ROWS * q : ROWS * (q + 1), :] = w_ref[own_columns(q), :]
        wp[c, z, y] = pack[...].astype(BF16)

    first_lane = ROWS * f - 128 * window_start(z)
    spot = lax.broadcasted_iota(jnp.int32, (ROWS, 128), 0) + first_lane
    lane = lax.broadcasted_iota(jnp.int32, (ROWS, 128), 1)

    def place_gains():
        gains_in.wait()
        gain_own = jnp.broadcast_to(gains_ref[...].astype(BF16), (8, ROWS))
        g0[c] = jnp.zeros((8, 128), F32)
        for r in range(3):
            hot = jnp.where(spot == lane + 128 * r, 1.0, 0.0).astype(BF16)
            g0[c, r : r + 1, :] = jnp.dot(gain_own, hot, preferred_element_type=F32)[0:1]

    def gain_twin(core):
        return remote(g0.at[core], g0.at[core], g0_s, g0_r, twin)

    def gain_y(kind):
        row = y if kind < 2 else yl
        return remote(g1.at[row], g1.at[row], g1_s.at[kind], g1_r.at[kind], left if kind == 1 else right)

    def gain_y_arrival(kind):
        row = (yl, yr, yo)[kind]
        return remote(g1.at[row], g1.at[row], g1_s.at[kind], g1_r.at[kind], right)

    def gain_z(direction, slab):
        ref = g2.at[slab]
        return remote(ref, ref, g2_s.at[direction, slab], g2_r.at[direction, slab], up if direction == 0 else down)

    def gain_chip():
        gain_twin(1 - c).wait_recv()
        g1[y] = g0[0] + g0[1]
        gain_y(0).start()
        gain_y(1).start()

    def gain_near():
        gain_y_arrival(0).wait_recv()
        gain_y(2).start()

    def gain_slab():
        gain_y_arrival(1).wait_recv()
        gain_y_arrival(2).wait_recv()
        g2[z] = total(g1, NY)
        both_ways(lambda direction: gain_z(direction, z).start())

    def gather_gain(t):
        for direction, slab, here, more in ((0, z - t, z - t >= 0, z < NZ - 1), (1, z + t, z + t <= NZ - 1, z > 0)):
            @pl.when(here)
            def _():
                gain_z(direction, slab).wait_recv()

                @pl.when(more)
                def _():
                    gain_z(direction, slab).start()

    def snap_x(kind):
        row = x if kind < 2 else xl
        return remote(sx.at[row], sx.at[row], sx_s.at[kind], sx_r.at[kind], x_left if kind == 1 else x_right)

    def snap_x_arrival(kind):
        row = (xl, xr, xo)[kind]
        return remote(sx.at[row], sx.at[row], sx_s.at[kind], sx_r.at[kind], x_right)

    def place_snapshot():
        snap_in.wait()
        sx[x] = jnp.zeros((40, 128), F32)
        sx[x, 0:ROWS, :] = snap_ref[...].reshape(ROWS, 128)
        snap_x(0).start()
        snap_x(1).start()

    def snapshot_near():
        snap_x_arrival(0).wait_recv()
        snap_x(2).start()

    def pass_token(t):
        if t > 0:
            pl.semaphore_wait(token.at[t - 1], 1)
        if t < NZ - 1:
            pl.semaphore_signal(token.at[t], inc=1, device_id=after, device_id_type=MESH)

    def barrier_wait():
        pl.semaphore_wait(barrier, len(peers))

    def spread_start(buf, own, peer_list, send, recv, src=None):
        for index, peer in peer_list:
            source = buf.at[own] if src is None else src.at[index]
            remote(source, buf.at[own], send.at[index], recv.at[own], peer).start()

    def spread_wait(buf, own, peer_list, send, recv):
        for index, peer in peer_list:
            remote(buf.at[index], buf.at[index], send.at[index], recv.at[index], peer).wait_recv()

    def spread_done(buf, own, peer_list, send, recv, src=None):
        for index, peer in peer_list:
            source = buf.at[own] if src is None else src.at[index]
            remote(source, buf.at[own], send.at[index], recv.at[own], peer).wait_send()

    def total(buf, count):
        result = buf[0]
        for index in range(1, count):
            result = result + buf[index]
        return result

    first = pl.ds(0, 2 * ZH)
    halves = (pl.ds(0, ZH), pl.ds(ZH, ZH))
    final = pl.ds(2 * ZH, VR)

    def z_copy(direction, slab):
        ref = wp.at[c, slab, y, first]
        return remote(
            ref, ref, agz_s.at[direction, slab], agz_r.at[direction, slab], up_two if direction == 0 else down_two
        )

    def mate_copy(slab):
        ref = wp.at[c, slab, y, first]
        return remote(ref, ref, agp_s.at[slab], agp_r.at[slab], mate)

    def v_copy(direction, slab, yy):
        ref = wp.at[c, slab, yy, final]
        return remote(
            ref, ref, agv_s.at[direction, slab, yy], agv_r.at[direction, slab, yy], up if direction == 0 else down
        )

    def y_copy(kind, slab):
        device = right if kind in (0, 2) else left
        if kind < 2:
            ref = wp.at[c, slab, y, first]
        elif kind == 2:
            ref = wp.at[c, slab, yl, halves[0]]
        else:
            ref = wp.at[c, slab, yr, halves[1]]
        return remote(ref, ref, ay_s.at[kind, slab], ay_r.at[kind, slab], device)

    def y_arrival(kind, slab):
        ref = [
            wp.at[c, slab, yl, first], wp.at[c, slab, yr, first], wp.at[c, slab, yo, halves[0]],
            wp.at[c, slab, yo, halves[1]],
        ][kind]
        return remote(ref, ref, ay_s.at[kind, slab], ay_r.at[kind, slab], right)

    low, high = pl.ds(0, VH), pl.ds(VH, VH)
    final_low, final_high = pl.ds(2 * ZH, VH), pl.ds(2 * ZH + VH, VH)

    def vy_copy(kind):
        device = right if kind in (0, 2) else left
        if kind < 2:
            ref = wp.at[c, z, y, final]
        elif kind == 2:
            ref = wp.at[c, z, yl, final_low]
        else:
            ref = wp.at[c, z, yr, final_high]
        return remote(ref, ref, av_s.at[kind], av_r.at[kind], device)

    def vy_arrival(kind):
        ref = [
            wp.at[c, z, yl, final], wp.at[c, z, yr, final], wp.at[c, z, yo, final_low], wp.at[c, z, yo, final_high],
        ][kind]
        return remote(ref, ref, av_s.at[kind], av_r.at[kind], right)

    def twin_copy(slab, core):
        return remote(wp.at[core, slab], wp.at[core, slab], tw_s.at[slab], tw_r.at[slab], twin)

    def both_ways(send):
        @pl.when(z < NZ - 1)
        def _():
            send(0)

        @pl.when(z > 0)
        def _():
            send(1)

    def both_ways_two(send):
        @pl.when(pair < pairs - 1)
        def _():
            send(0)

        @pl.when(pair > 0)
        def _():
            send(1)

    def gather_own():
        vy_copy(0).start()
        vy_copy(1).start()
        both_ways_two(lambda direction: z_copy(direction, z).start())
        mate_copy(z).start()
        both_ways(lambda direction: v_copy(direction, z, y).start())
        y_copy(0, z).start()
        y_copy(1, z).start()

    def gather_near():
        vy_arrival(0).wait_recv()
        vy_copy(2).start()
        both_ways(lambda direction: v_copy(direction, z, yl).start())
        vy_arrival(1).wait_recv()
        vy_copy(3).start()
        both_ways(lambda direction: v_copy(direction, z, yr).start())

    def gather_far():
        vy_arrival(2).wait_recv()
        vy_arrival(3).wait_recv()
        both_ways(lambda direction: v_copy(direction, z, yo).start())

    v_order = (y, yl, yr, yo)

    def gather_z(t):
        for direction, slab, here, more in (
            (0, z - 2 * t, pair >= t, pair < pairs - 1), (1, z + 2 * t, pair + t < pairs, pair > 0),
        ):
            @pl.when(here)
            def _():
                z_copy(direction, slab).wait_recv()

                @pl.when(more)
                def _():
                    z_copy(direction, slab).start()

                mate_copy(slab).start()
                y_copy(0, slab).start()
                y_copy(1, slab).start()

    def gather_mate(t):
        sides = ((z_mate, pair >= 0),) if t == 0 else ((z_mate - 2 * t, pair >= t), (z_mate + 2 * t, pair + t < pairs))
        for slab, here in sides:
            @pl.when(here)
            def _():
                mate_copy(slab).wait_recv()
                y_copy(0, slab).start()
                y_copy(1, slab).start()

    def gather_v(t):
        for direction, slab, here, more in ((0, z - t, z - t >= 0, z < NZ - 1), (1, z + t, z + t <= NZ - 1, z > 0)):
            @pl.when(here)
            def _():
                for yy in v_order:
                    v_copy(direction, slab, yy).wait_recv()

                    @pl.when(more)
                    def _():
                        v_copy(direction, slab, yy).start()

    def gather_y(j):
        slab = order(z, 7 - j)
        y_arrival(0, slab).wait_recv()
        y_copy(2, slab).start()
        y_arrival(1, slab).wait_recv()
        y_copy(3, slab).start()

    def gather_twin(j):
        slab = order(z, 7 - j)
        y_arrival(2, slab).wait_recv()
        y_arrival(3, slab).wait_recv()
        twin_copy(slab, c).start()

    def unpack(lo, hi):
        def one(j, _):
            slab = order(z, 7 - j)
            twin_copy(slab, 1 - c).wait_recv()
            for core in range(2):
                for yy in range(NY):
                    block = wp[core, slab, yy].astype(F32)
                    base = ROWS * (2 * yy + core)
                    for q in range(FRAGS):
                        stage[base : base + ROWS, 128 * q : 128 * (q + 1)] = block[ROWS * q : ROWS * (q + 1)]
            w[pl.ds(pl.multiple_of(SLAB * slab, 16), SLAB), :] = stage[...].astype(BF16)
            return 0

        lax.fori_loop(lo, hi, one, 0)

    def normalise(lo, hi):
        def one(r, _):
            rows = pl.ds(pl.multiple_of(32 * r, 32), 32)
            tokens = hid[rows, :].astype(F32)
            inverse = lax.rsqrt(jnp.sum(tokens * tokens, axis=-1, keepdims=True) / D + epsilon)
            invb[rows, :] = jnp.broadcast_to(inverse, (32, 128))
            nbx[c, rows, :] = (tokens * inverse).astype(BF16)
            return 0

        lax.fori_loop(lo, hi, one, 0)

    def gain_vector():
        grow[...] = jnp.zeros((8, D), F32)
        for slab in range(NZ):
            for r in range(3):
                lanes = slice(128 * (window_start(slab) + r), 128 * (window_start(slab) + r + 1))
                grow[0:1, lanes] = grow[0:1, lanes] + g2[slab, r : r + 1, :]

    def apply_gain():
        def one(r, _):
            rows = pl.ds(pl.multiple_of(32 * r, 32), 32)
            normed = hid[rows, :].astype(F32) * invb[rows, 0:1]
            nbg[rows, :] = (normed * grow[0:1, :]).astype(BF16)
            return 0

        lax.fori_loop(0, TOK // 32, one, 0)

    def nx_nb(core, half):
        ref = nbx.at[core, pl.ds(half * TOK // 2, TOK // 2)]
        return remote(ref, ref, nx_s.at[half], nx_r.at[half], twin)

    def nx_gv(core):
        return remote(gx.at[core], gx.at[core], nx_s.at[2], nx_r.at[2], twin)

    def weight_terms(core, lo, hi):
        columns = pl.ds(pl.multiple_of(HALF * c, 128), HALF)

        def one(k, _):
            feats = pl.ds(pl.multiple_of(256 * k, 256), 256)
            terms = lax.dot_general(
                nbx[core, :, feats], gx[core, :, columns], (((0,), (0,)), ((), ())), preferred_element_type=F32
            )
            dw[feats, :] = terms if core is c else dw[feats, :] + terms
            return 0

        lax.fori_loop(lo, hi, one, 0)

    def term(slab, yy, row, count):
        base = pl.multiple_of(CHIP * (NY * slab + yy), 8)
        parts, end = [], row + count
        while row < end:
            q, r = row // CHIP, row % CHIP
            count = min(CHIP - r, end - row)
            parts.append(dw[pl.ds(base + r, count), 128 * q : 128 * (q + 1)])
            row += count
        return jnp.concatenate(parts, axis=0)

    def far_copy(kind, slab):
        return remote(
            s1.at[slab, kind], r1.at[slab, kind], ry_s.at[kind, slab], ry_r.at[kind, slab], right if kind == 0 else left
        )

    def near_copy(kind, slab):
        return remote(
            s2.at[slab, kind], r2.at[slab, kind], ry_s.at[2 + kind, slab], ry_r.at[2 + kind, slab],
            right if kind == 0 else left,
        )

    def chain_copy(direction, slab):
        return remote(
            sz.at[slab], rz.at[direction, slab], rz_s.at[direction, slab], rz_r.at[direction, slab],
            up_two if direction == 0 else down_two,
        )

    def pair_copy(slab):
        return remote(sp.at[slab // 2], rp.at[slab // 2], rp_s.at[slab // 2], rp_r.at[slab // 2], mate)

    def reduce_pair(i):
        slab = order(z, 2 * i)
        sp[slab // 2] = racc[slab].astype(BF16)
        pair_copy(slab).start()

    def reduce_pair_wait(i):
        slab = order(z, 2 * i + 1)
        pair_copy(slab).wait_recv()
        racc[slab] = racc[slab] + rp[slab // 2].astype(F32)

    def chain_v_copy(direction, slab, yy):
        return remote(
            vz.at[slab, yy], rv.at[direction, slab, yy], rv_s.at[direction, slab, yy], rv_r.at[direction, slab, yy],
            up if direction == 0 else down,
        )

    def reduce_far(s):
        slab = order(z, s)
        for kind in range(2):
            s1[slab, kind] = term(slab, yo, ZH * kind, ZH).astype(BF16)
            far_copy(kind, slab).start()

    def reduce_near(s):
        slab = order(z, s)
        for kind, yy in ((0, yr), (1, yl)):
            far_copy(kind, slab).wait_recv()
            s2[slab, kind, kind] = (term(slab, yy, ZH * kind, ZH) + r1[slab, kind].astype(F32)).astype(BF16)
            s2[slab, kind, 1 - kind] = term(slab, yy, ZH * (1 - kind), ZH).astype(BF16)
            near_copy(kind, slab).start()

    def reduce_row(s):
        slab = order(z, s)
        near_copy(0, slab).wait_recv()
        near_copy(1, slab).wait_recv()
        for p in range(2):
            racc[slab, p] = term(slab, y, ZH * p, ZH) + r2[slab, 0, p].astype(F32) + r2[slab, 1, p].astype(F32)

    def reduce_chain(u):
        reduce_pair_wait(u)
        if u == pairs - 1:
            for direction, here in ((0, pair > 0), (1, pair < pairs - 1)):
                @pl.when(here)
                def _():
                    chain_copy(direction, z).wait_recv()
                    racc[z] = racc[z] + rz[direction, z].astype(F32)

            return

        far = pairs - 1 - u
        for direction, slab, here, later in (
            (0, z + 2 * far, pair <= u, pair > 0), (1, z - 2 * far, pair >= far, pair < pairs - 1),
        ):
            @pl.when(here)
            def _():
                @pl.when(later)
                def _():
                    chain_copy(direction, slab).wait_recv()
                    sz[slab] = (racc[slab] + rz[direction, slab].astype(F32)).astype(BF16)

                @pl.when(jnp.logical_not(later))
                def _():
                    sz[slab] = racc[slab].astype(BF16)

                chain_copy(direction, slab).start()

    def reduce_v(u):
        if u == NZ - 1:
            for k in (2, 1, 3, 0):
                yy = (y + k) % NY
                vacc[k] = term(z, yy, 2 * ZH, VR)
                for direction, here in ((0, z > 0), (1, z < NZ - 1)):
                    @pl.when(here)
                    def _():
                        chain_v_copy(direction, z, yy).wait_recv()
                        vacc[k] = vacc[k] + rv[direction, z, yy].astype(F32)

                if k == 2:
                    vs1[...] = vacc[2].astype(BF16)
                    v_far(0).start()
                    v_far(1).start()
            return

        for direction, slab, here, later in (
            (0, NZ - 1 + z - u, z <= u, z > 0), (1, z - (NZ - 1) + u, z >= NZ - 1 - u, z < NZ - 1),
        ):
            @pl.when(here)
            def _():
                for k in (2, 1, 3, 0):
                    yy = (y + k) % NY

                    @pl.when(later)
                    def _():
                        chain_v_copy(direction, slab, yy).wait_recv()
                        vz[slab, yy] = (term(slab, yy, 2 * ZH, VR) + rv[direction, slab, yy].astype(F32)).astype(BF16)

                    @pl.when(jnp.logical_not(later))
                    def _():
                        vz[slab, yy] = term(slab, yy, 2 * ZH, VR).astype(BF16)

                    chain_v_copy(direction, slab, yy).start()

    def v_far(kind):
        part = low if kind == 0 else high
        return remote(vs1.at[part], vr1.at[part], vy_s.at[kind], vy_r.at[kind], right if kind == 0 else left)

    def v_near(kind):
        return remote(vs2.at[kind], vr2.at[kind], vy_s.at[2 + kind], vy_r.at[2 + kind], right if kind == 0 else left)

    def reduce_v_near():
        v_far(0).wait_recv()
        vs2[0] = jnp.concatenate(
            [vacc[1, 0:VH] + vr1[0:VH].astype(F32), vacc[1, VH:VR]], axis=0
        ).astype(BF16)
        v_near(0).start()
        v_far(1).wait_recv()
        vs2[1] = jnp.concatenate(
            [vacc[3, 0:VH], vacc[3, VH:VR] + vr1[VH:VR].astype(F32)], axis=0
        ).astype(BF16)
        v_near(1).start()

    def reduce_v_row():
        v_near(0).wait_recv()
        v_near(1).wait_recv()
        fbuf[c, 2 * ZH : BLOCK] = vacc[0] + vr2[0].astype(F32) + vr2[1].astype(F32)

    def make_values():
        def one(n, _):
            columns = pl.ds(pl.multiple_of(256 * n, 256), 256)
            vout[:, columns] = (jnp.dot(nbg[...], w[:, columns], preferred_element_type=F32) * FACTOR).astype(BF16)
            return 0

        lax.fori_loop(0, KV // 256, one, 0)

    def input_gradient(lo, hi):
        def one(k, _):
            feats = pl.ds(pl.multiple_of(256 * k, 256), 256)
            ig[:, feats] = (
                lax.dot_general(gx[c], w[feats, :], (((1,), (1,)), ((), ())), preferred_element_type=F32) * FACTOR
            )
            return 0

        lax.fori_loop(lo, hi, one, 0)

    def hidden_gradient(lo, hi):
        def one(r, _):
            rows = pl.ds(pl.multiple_of(32 * r, 32), 32)
            inverse = invb[rows, 0:1]
            normed = hid[rows, :].astype(F32) * inverse
            grad = ig[rows, :]
            along = grad * normed
            gacc[...] += jnp.sum(along.reshape(4, 8, D), axis=0)
            gain = grow[0:1, :]
            mean = jnp.sum(along * gain, axis=-1, keepdims=True) / D
            gh[rows, :] = (inverse * (grad * gain - normed * mean)).astype(BF16)
            return 0

        lax.fori_loop(lo, hi, one, 0)

    def gain_terms():
        gain_row = jnp.sum(gacc[...], axis=0, keepdims=True)
        hsrc[...] = jnp.zeros((NZ, 8, 128), F32)
        for slab in range(NZ):
            for r in range(3):
                lanes = slice(128 * (window_start(slab) + r), 128 * (window_start(slab) + r + 1))
                hsrc[slab, r : r + 1, :] = gain_row[:, lanes]
        h1[z] = hsrc[z]
        spread_start(h1, z, z_peers, h1_s, h1_r, src=hsrc)

    def gain_second():
        spread_wait(h1, z, z_peers, h1_s, h1_r)
        h2[e] = total(h1, NZ)
        spread_start(h2, e, e_peers, h2_s, h2_r)

    def gain_step():
        spread_wait(h2, e, e_peers, h2_s, h2_r)
        window = total(h2, NE)
        gain_grad = jnp.zeros((8, ROWS), F32)
        for r in range(3):
            hot = jnp.where(spot == lane + 128 * r, 1.0, 0.0)
            gain_grad = gain_grad + lax.dot_general(
                jnp.broadcast_to(window[r : r + 1], (8, 128)), hot, (((1,), (1,)), ((), ())),
                precision=lax.Precision.HIGHEST, preferred_element_type=F32,
            )
        newg_ref[...] = gains_ref[...] - gain_rate * gain_grad[0:1]
        out(3).start()

    def snapshot_second():
        snap_x_arrival(1).wait_recv()
        snap_x_arrival(2).wait_recv()
        szh[zh] = total(sx, NX)
        szh_copy(zh).start()

    def szh_copy(half):
        return remote(szh.at[half], szh.at[half], szh_s, szh_r, zh_peer)

    def outer_step():
        outer_in.wait()
        mom_in.wait()
        szh_copy(1 - zh).wait_recv()
        change = outer_ref[...] - (szh[0] + szh[1])[0:ROWS] / (2 * NX)
        new_moment = momentum * mom_ref[...] + change
        newm_ref[...] = new_moment
        newo_ref[...] = outer_ref[...] - outer_rate * (change + momentum * new_moment)
        out(4).start()
        out(5).start()

    def last(core):
        return remote(fbuf.at[core], fbuf.at[core], f_s, f_r, twin)

    def inner_step():
        last(1 - c).wait_recv()
        row_of = lax.broadcasted_iota(jnp.int32, (ROWS, ROWS), 0)
        column_of = lax.broadcasted_iota(jnp.int32, (ROWS, ROWS), 1)
        gain_bf = jnp.broadcast_to(gains_ref[...].astype(BF16).astype(F32), (ROWS, ROWS))
        scale = jnp.sum(jnp.where(row_of == column_of, gain_bf, 0.0), axis=1, keepdims=True) * FACTOR
        for core in range(2):
            @pl.when(c == core)
            def _():
                for j in range(FRAGS):
                    row = CHIP * (j % 4) + ROWS * core
                    grad = fbuf[j // 4, row : row + ROWS, :] * scale
                    inner = w_ref[own_columns(j), :] - inner_rate * grad
                    mixed = mixing * inner + (1.0 - mixing) * newo_ref[...]
                    neww_ref[own_columns(j), :] = jnp.where(frag_ref[0] == j, mixed, inner)

        out(2).start()

    results = (
        (vout, values_hbm), (gh, gh_hbm), (neww_ref, neww_hbm), (newg_ref, newg_hbm), (newo_ref, newo_hbm),
        (newm_ref, newm_hbm),
    )

    def out(index):
        return pltpu.make_async_copy(results[index][0], results[index][1], out_sem.at[index])

    def drain():
        for t in range(NZ):
            for direction, slab, here in (
                (0, z - t, jnp.logical_and(z - t >= 0, z < NZ - 1)), (1, z + t, jnp.logical_and(z + t <= NZ - 1, z > 0)),
            ):
                @pl.when(here)
                def _():
                    gain_z(direction, slab).wait_send()
                    for yy in range(NY):
                        v_copy(direction, slab, yy).wait_send()

        for t in range(pairs):
            for direction, slab, here in (
                (0, z - 2 * t, jnp.logical_and(pair >= t, pair < pairs - 1)),
                (1, z + 2 * t, jnp.logical_and(pair + t < pairs, pair > 0)),
            ):
                @pl.when(here)
                def _():
                    z_copy(direction, slab).wait_send()

        def one(slab, _):
            for kind in range(4):
                y_copy(kind, slab).wait_send()
            twin_copy(slab, c).wait_send()
            for kind in range(2):
                far_copy(kind, slab).wait_send()
                near_copy(kind, slab).wait_send()

            for direction, here in ((0, slab > z), (1, slab < z)):
                @pl.when(here)
                def _():
                    for yy in range(NY):
                        chain_v_copy(direction, slab, yy).wait_send()

                @pl.when(jnp.logical_and(here, slab % 2 == z % 2))
                def _():
                    chain_copy(direction, slab).wait_send()

            @pl.when(slab % 2 == z % 2)
            def _():
                mate_copy(slab).wait_send()

            @pl.when(slab % 2 != z % 2)
            def _():
                pair_copy(slab).wait_send()

            return 0

        lax.fori_loop(0, NZ, one, 0)
        for kind in range(4):
            vy_copy(kind).wait_send()
        for kind in range(2):
            v_far(kind).wait_send()
            v_near(kind).wait_send()
        nx_nb(c, 0).wait_send()
        nx_nb(c, 1).wait_send()
        nx_gv(c).wait_send()
        last(c).wait_send()
        szh_copy(zh).wait_send()
        gain_twin(c).wait_send()
        for kind in range(3):
            gain_y(kind).wait_send()
            snap_x(kind).wait_send()
        spread_done(h1, z, z_peers, h1_s, h1_r, src=hsrc)

    place_gains()
    pack_own()
    barrier_wait()
    gain_twin(c).start()
    gather_own()
    pass_token(0)
    gv_in.wait()
    nx_gv(c).start()
    hid_in.wait()
    normalise(0, 4)
    nx_nb(c, 0).start()
    normalise(4, 8)
    nx_nb(c, 1).start()
    gain_chip()
    place_snapshot()
    gather_near()
    weight_terms(c, 0, 5)
    gather_far()
    gather_mate(0)
    gather_z(1)
    weight_terms(c, 5, 9)
    gather_v(1)
    gather_y(0)
    pass_token(1)
    gain_near()
    nx_gv(1 - c).wait_recv()
    nx_nb(1 - c, 0).wait_recv()
    nx_nb(1 - c, 1).wait_recv()
    weight_terms(1 - c, 0, 5)
    gather_y(1)
    gather_mate(1)
    weight_terms(1 - c, 5, 9)
    gather_z(2)
    gather_v(2)
    reduce_v(0)
    reduce_far(0)
    reduce_far(1)
    gain_slab()
    snapshot_near()
    pass_token(2)
    gather_v(3)
    gather_y(2)
    gather_mate(2)
    gather_twin(0)
    reduce_v(1)
    gather_z(3)
    gather_y(3)
    gather_twin(1)
    reduce_near(0)
    reduce_near(1)
    reduce_far(2)
    reduce_far(3)
    pass_token(3)
    gather_gain(1)
    gather_v(4)
    reduce_v(2)
    gather_mate(3)
    gather_y(4)
    gather_twin(2)
    reduce_row(0)
    reduce_row(1)
    reduce_pair(0)
    reduce_near(2)
    reduce_near(3)
    pass_token(4)
    gather_gain(2)
    gather_v(5)
    reduce_v(3)
    gather_y(5)
    gather_twin(3)
    reduce_far(4)
    reduce_far(5)
    reduce_chain(0)
    pass_token(5)
    gather_gain(3)
    gather_v(6)
    reduce_v(4)
    gather_y(6)
    gather_twin(4)
    unpack(0, 2)
    reduce_row(2)
    reduce_row(3)
    reduce_pair(1)
    reduce_near(4)
    reduce_near(5)
    reduce_far(6)
    reduce_far(7)
    pass_token(6)
    gather_gain(4)
    gather_v(7)
    gather_y(7)
    gather_twin(5)
    reduce_v(5)
    reduce_chain(1)
    pass_token(7)
    snapshot_second()
    gather_twin(6)
    unpack(2, 4)
    reduce_row(4)
    reduce_row(5)
    reduce_pair(2)
    reduce_near(6)
    reduce_near(7)
    gather_gain(5)
    gather_twin(7)
    reduce_v(6)
    gather_gain(6)
    unpack(4, 6)
    reduce_chain(2)
    gather_gain(7)
    gain_vector()
    reduce_v(7)
    apply_gain()
    reduce_row(6)
    reduce_row(7)
    reduce_pair(3)
    unpack(6, 8)
    input_gradient(0, 5)
    reduce_v_near()
    input_gradient(5, 9)
    reduce_chain(3)
    fbuf[c, 0 : 2 * ZH] = racc[z].reshape(2 * ZH, 128)
    gacc[...] = jnp.zeros((8, D), F32)
    hidden_gradient(0, 8)
    out(1).start()
    gain_terms()
    reduce_v_row()
    last(c).start()
    make_values()
    out(0).start()
    outer_step()
    inner_step()
    gain_second()
    drain()
    gain_step()
    spread_done(h2, e, e_peers, h2_s, h2_r)
    for index in range(6):
        out(index).wait()


def place_kernel(*refs):
    sources, targets, held, in_sem, out_sem = refs[:6], refs[6:12], refs[12:18], refs[18], refs[19]
    arrive = [pltpu.make_async_copy(s, t, in_sem.at[i]) for i, (s, t) in enumerate(zip(sources, held))]
    leave = [pltpu.make_async_copy(s, t, out_sem.at[i]) for i, (s, t) in enumerate(zip(held, targets))]
    for copy in arrive:
        copy.start()
    for one, other in zip(arrive, leave):
        one.wait()
        other.start()
    for copy in leave:
        copy.wait()


def body(hidden, grad_values, weights, gains, snapshot, outer_frag, outer_moment, fragment_index):
    anywhere = pl.BlockSpec(memory_space=pl.ANY)
    dma = pltpu.SemaphoreType.DMA
    vmem = pltpu.VMEM
    shapes = (
        jax.ShapeDtypeStruct((TOK, KV), BF16),
        jax.ShapeDtypeStruct((TOK, D), BF16),
        jax.ShapeDtypeStruct((ROWS * FRAGS, 128), F32),
        jax.ShapeDtypeStruct((1, ROWS), F32),
        jax.ShapeDtypeStruct((ROWS, FW), F32),
        jax.ShapeDtypeStruct((ROWS, FW), F32),
    )
    results = pl.pallas_call(
        step_kernel,
        out_shape=shapes,
        in_specs=[pl.BlockSpec(memory_space=pltpu.SMEM)] + [anywhere] * 7,
        out_specs=(anywhere,) * 6,
        scratch_shapes=[
            vmem((TOK, D), BF16),
            vmem((2, TOK, KV), BF16),
            vmem((2, TOK, D), BF16),
            vmem((TOK, D), BF16),
            vmem((2, NZ, NY, BLOCK, 128), BF16),
            vmem((D, KV), BF16),
            vmem((SLAB, KV), F32),
            vmem((BLOCK, 128), F32),
            vmem((D, HALF), F32),
            vmem((NZ, 2, ZH, 128), BF16),
            vmem((NZ, 2, ZH, 128), BF16),
            vmem((NZ, 2, 2, ZH, 128), BF16),
            vmem((NZ, 2, 2, ZH, 128), BF16),
            vmem((NZ, 2, ZH, 128), F32),
            vmem((NZ // 2, 2, ZH, 128), BF16),
            vmem((NZ // 2, 2, ZH, 128), BF16),
            vmem((NZ, 2, ZH, 128), BF16),
            vmem((2, NZ, 2, ZH, 128), BF16),
            vmem((NY, VR, 128), F32),
            vmem((VR, 128), BF16),
            vmem((VR, 128), BF16),
            vmem((2, VR, 128), BF16),
            vmem((2, VR, 128), BF16),
            vmem((NZ, NY, VR, 128), BF16),
            vmem((2, NZ, NY, VR, 128), BF16),
            vmem((2, BLOCK, 128), F32),
            vmem((TOK, D), F32),
            vmem((TOK, KV), BF16),
            vmem((TOK, D), BF16),
            vmem((TOK, 128), F32),
            vmem((8, D), F32),
            vmem((8, D), F32),
            vmem((2, 8, 128), F32),
            vmem((NY, 8, 128), F32),
            vmem((NZ, 8, 128), F32),
            vmem((NZ, 8, 128), F32),
            vmem((NZ, 8, 128), F32),
            vmem((NE, 8, 128), F32),
            vmem((NX, 40, 128), F32),
            vmem((2, 40, 128), F32),
            vmem((ROWS * FRAGS, 128), F32),
            vmem((1, ROWS), F32),
            vmem((ROWS, 1, FW), F32),
            vmem((ROWS, FW), F32),
            vmem((ROWS, FW), F32),
            vmem((ROWS * FRAGS, 128), F32),
            vmem((1, ROWS), F32),
            vmem((ROWS, FW), F32),
            vmem((ROWS, FW), F32),
            dma((7,)), dma((6,)),
            dma((2, NZ)), dma((2, NZ)),
            dma((NZ,)), dma((NZ,)),
            dma((2, NZ, NY)), dma((2, NZ, NY)),
            dma((4, NZ)), dma((4, NZ)),
            dma((4,)), dma((4,)),
            dma((NZ,)), dma((NZ,)),
            dma((3,)), dma((3,)),
            dma((4, NZ)), dma((4, NZ)),
            dma((NZ // 2,)), dma((NZ // 2,)),
            dma((2, NZ)), dma((2, NZ)),
            dma((2, NZ, NY)), dma((2, NZ, NY)),
            dma((4,)), dma((4,)),
            dma, dma,
            dma, dma,
            dma((3,)), dma((3,)),
            dma((2, NZ)), dma((2, NZ)),
            dma((NZ,)), dma((NZ,)),
            dma((NE,)), dma((NE,)),
            dma((3,)), dma((3,)),
            dma, dma,
            pltpu.SemaphoreType.REGULAR((7,)),
        ],
        compiler_params=pltpu.CompilerParams(
            collective_id=0, has_side_effects=True, vmem_limit_bytes=56 * 1024 * 1024
        ),
        cost_estimate=pl.CostEstimate(flops=3 * 2 * TOK * D * KV, bytes_accessed=4_000_000, transcendentals=0),
    )(
        fragment_index, hidden, grad_values, weights.reshape(ROWS * FRAGS, 128), gains,
        snapshot.reshape(ROWS, 1, FW), outer_frag, outer_moment,
    )
    values, grad_hidden, new_weights, new_gains, new_outer, new_moment = pl.pallas_call(
        place_kernel,
        out_shape=shapes,
        in_specs=[anywhere] * 6,
        out_specs=(anywhere,) * 6,
        scratch_shapes=[vmem(shape.shape, shape.dtype) for shape in shapes] + [dma((6,)), dma((6,))],
        compiler_params=pltpu.CompilerParams(vmem_limit_bytes=60 * 1024 * 1024),
    )(*results)
    return (values, grad_hidden, new_weights.reshape(1, ROWS, KV), new_gains, new_outer, new_moment)


def solution(mesh):
    return jax.shard_map(
        body,
        mesh=mesh,
        in_specs=(
            P(("group", "fsdp"), None),
            P(("group", "fsdp"), None),
            P("group", "fsdp", None),
            P("group", "fsdp"),
            P("group", "fsdp", None),
            P("fsdp", None),
            P("fsdp", None),
            P(),
        ),
        out_specs=(
            P(("group", "fsdp"), None),
            P(("group", "fsdp"), None),
            P("group", "fsdp", None),
            P("group", "fsdp"),
            P("fsdp", None),
            P("fsdp", None),
        ),
        check_vma=False,
    )
```

time: 1080 us -> 80.9 us (0.07)
  blocking collectives: 709 us -> 0 us
  waiting for transfers between devices: 227 us -> 0 us
  Pallas kernels: 0 us -> 79.4 us
  starting transfers between devices: 60.3 us -> 0 us
  matrix products: 23.6 us -> 0 us
  local copies, waits for them, and re-layouts: 23.1 us -> 0 us
  between operations: 16.3 us -> 1.29 us
  other arithmetic: 13.5 us -> 0 us
    unnamed x2 -> x0, blocking collectives: 637 us -> none
    all_to_all x8 -> x0, waiting for transfers between devices: 227 us -> none  [weight_gradient(): lax.all_to_all(partial_sum.astype(jnp.bfloat16), 'fsdp', split_axis=0, co...]
    pallas_call x0 -> x2, Pallas kernels: none -> 79.4 us  [the longest x1 76.8 us: body(): pl.pallas_call(step_kernel, out_shape=shapes, in_specs=[pl.BlockSpec(memo...]
    psum x1 -> x0, blocking collectives: 72.4 us -> none  [synchronise(): summed = lax.psum(snapshot[0], 'group')]
    all_to_all x8 -> x0, starting transfers between devices: 60.3 us -> none  [weight_gradient(): lax.all_to_all(partial_sum.astype(jnp.bfloat16), 'fsdp', split_axis=0, co...]
    dot_general x10 -> x0, matrix products: 23.6 us -> none  [the longest x8 16.5 us: weight_gradient(): lax.dot_general(normed_bf, cotangent, (((0,), (0,)), ((), ())), preferred...]
    convert_element_type x8 -> x0, local copies, waits for them, and re-layouts: 12.7 us -> none  [weight_gradient(): partial_sum.astype(jnp.bfloat16)]
  transfers between devices with their start and end apart: 9 -> 0, of which waited for: 7 -> 0; matrix products, arithmetic and copies ran while one was open for 3% -> 0% of each run, Pallas kernels for 0% -> 0%
where the time goes in v2:
time: 80.9 us; the launch traced here: 80.7 us
  Pallas kernels  79.4 us (98%)
  between operations  1.29 us (2%)
    pallas_call x1, Pallas kernels, body(): pl.pallas_call(step_kernel, out_shape=shapes, in_specs=[pl.BlockSpec(memo...  76.8 us
    pallas_call x1, Pallas kernels, body(): pl.pallas_call(place_kernel, out_shape=shapes, in_specs=[anywhere] * 6, o...  2.6 us

profile of v2, /device:TPU:1, one launch (start us, length us, event | category | flops | bytes accessed | tf_op | source)
XLA Modules:
  0.0 80.7 jit_solution(3004142762363952209)
XLA Ops:
  1.3 76.8 %shard_map.127 = (bf16[256,1024]{1,0:T(8,128)(2,1)}, bf16[256,2304]{1,0:T(8,128)(2,1)}, f32[288,128]{1,0:T(8,128)}, f32[1,36]{1,0:T(1,128)}, f32[36,128]{1,0:T(8,128)}, /*index=5*/f32[36,128]{1,0:T(8,128)}) custom-call(s32[1]{0:T(128)S(6)} %copy.16.frag_ref, bf16[256,2304]{1,0:T(8,128)(2,1)} %hid_hbm.1, bf16[256,1024]{1,0:T(8,128)(2,1)} %gv_hbm.1, ...), custom_call_target="tpu_custom_call" | custom-call | flops 3623878656 | bytes 4000000 | tf_op jit(solution)/shard_map/pallas_call | solution.py:927
  78.1 2.6 %shard_map.128 = (bf16[256,1024]{1,0:T(8,128)(2,1)}, bf16[256,2304]{1,0:T(8,128)(2,1)}, f32[288,128]{1,0:T(8,128)}, f32[1,36]{1,0:T(1,128)}, f32[36,128]{1,0:T(8,128)}, /*index=5*/f32[36,128]{1,0:T(8,128)}) custom-call(bf16[256,1024]{1,0:T(8,128)(2,1)} %get-tuple-element.18.refs_0_, bf16[256,2304]{1,0:T(8,128)(2,1)} %get-tuple-element.19.refs_1_, ...), custom_call_target="tpu_custom_call" | custom-call | tf_op jit(solution)/shard_map/pallas_call | solution.py:1013

commit v3 on v2

--- a/solution.py
+++ b/solution.py
@@ -33,6 +33,7 @@
 mixing = 0.5
 FACTOR = D ** (-0.5)
 BLOCK = 288
+AH = BLOCK // 2
 ZH = 112
 VR = 64
 VH = VR // 2
@@ -55,11 +56,11 @@
     values_hbm, gh_hbm, neww_hbm, newg_hbm, newo_hbm, newm_hbm,
     hid, gx, nbx, nbg, wp, w, stage, pack, dw, s1, r1, s2, r2, racc, sp, rp, sz, rz,
     vacc, vs1, vr1, vs2, vr2, vz, rv, fbuf,
-    ig, vout, gh, invb, grow, gacc, g0, g1, g2, hsrc, h1, h2, sx, szh,
+    ig, vf, vout, gh, invb, grow, gacc, g0, g1, g2, hsrc, h1, h2, sx, szh,
     w_ref, gains_ref, snap_ref, outer_ref, mom_ref, neww_ref, newg_ref, newo_ref, newm_ref,
-    in_sem, out_sem, agz_s, agz_r, agp_s, agp_r, agv_s, agv_r, ay_s, ay_r, av_s, av_r, tw_s, tw_r, nx_s, nx_r,
+    in_sem, out_sem, agz_s, agz_r, agp_s, agp_r, ay_s, ay_r, tw_s, tw_r, nx_s, nx_r,
     ry_s, ry_r, rp_s, rp_r, rz_s, rz_r, rv_s, rv_r, vy_s, vy_r, f_s, f_r,
-    g0_s, g0_r, g1_s, g1_r, g2_s, g2_r, h1_s, h1_r, h2_s, h2_r, sx_s, sx_r, szh_s, szh_r, token,
+    g0_s, g0_r, g1_s, g1_r, g2_s, g2_r, gm_s, gm_r, h1_s, h1_r, h2_s, h2_r, sx_s, sx_r, szh_s, szh_r, token,
 ):
     g = lax.axis_index("group")
     f = lax.axis_index("fsdp")
@@ -90,6 +91,12 @@
             src_ref=src, dst_ref=dst, send_sem=send, recv_sem=recv, device_id=device, device_id_type=MESH
         )
 
+    def received(ref, sem):
+        remote(ref, ref, sem, sem, twin).wait_recv()
+
+    def sent(ref, sem):
+        remote(ref, ref, sem, sem, twin).wait_send()
+
     barrier = pltpu.get_barrier_semaphore()
     peers = [before, after, right, left, x_right, x_left, twin]
     two_after, two_before = at((z + 2) % NZ, y), at((z + NZ - 2) % NZ, y)
@@ -133,15 +140,18 @@
 
     def gain_y(kind):
         row = y if kind < 2 else yl
-        return remote(g1.at[row], g1.at[row], g1_s.at[kind], g1_r.at[kind], left if kind == 1 else right)
-
-    def gain_y_arrival(kind):
-        row = (yl, yr, yo)[kind]
-        return remote(g1.at[row], g1.at[row], g1_s.at[kind], g1_r.at[kind], right)
+        return remote(
+            g1.at[row], g1.at[row], g1_s, g1_r.at[0 if kind == 0 else 1], left if kind == 1 else right
+        )
 
     def gain_z(direction, slab):
         ref = g2.at[slab]
-        return remote(ref, ref, g2_s.at[direction, slab], g2_r.at[direction, slab], up if direction == 0 else down)
+        return remote(
+            ref, ref, g2_s.at[direction, slab // 2], g2_r.at[slab // 2], up_two if direction == 0 else down_two
+        )
+
+    def gain_mate(slab):
+        return remote(g2.at[slab], g2.at[slab], gm_s, gm_r, mate)
 
     def gain_chip():
         gain_twin(1 - c).wait_recv()
@@ -150,17 +160,19 @@
         gain_y(1).start()
 
     def gain_near():
-        gain_y_arrival(0).wait_recv()
+        received(g1.at[yl], g1_r.at[0])
         gain_y(2).start()
 
     def gain_slab():
-        gain_y_arrival(1).wait_recv()
-        gain_y_arrival(2).wait_recv()
+        received(g1.at[pl.ds(0, 2)], g1_r.at[1])
         g2[z] = total(g1, NY)
-        both_ways(lambda direction: gain_z(direction, z).start())
+        both_ways_two(lambda direction: gain_z(direction, z).start())
+        gain_mate(z).start()
 
     def gather_gain(t):
-        for direction, slab, here, more in ((0, z - t, z - t >= 0, z < NZ - 1), (1, z + t, z + t <= NZ - 1, z > 0)):
+        for direction, slab, here, more in (
+            (0, z - 2 * t, pair >= t, pair < pairs - 1), (1, z + 2 * t, pair + t < pairs, pair > 0),
+        ):
             @pl.when(here)
             def _():
                 gain_z(direction, slab).wait_recv()
@@ -169,13 +181,16 @@
                 def _():
                     gain_z(direction, slab).start()
 
+                gain_mate(slab).start()
+
+    def gain_all():
+        received(g2.at[pl.ds(0, pairs)], gm_r)
+
     def snap_x(kind):
         row = x if kind < 2 else xl
-        return remote(sx.at[row], sx.at[row], sx_s.at[kind], sx_r.at[kind], x_left if kind == 1 else x_right)
-
-    def snap_x_arrival(kind):
-        row = (xl, xr, xo)[kind]
-        return remote(sx.at[row], sx.at[row], sx_s.at[kind], sx_r.at[kind], x_right)
+        return remote(
+            sx.at[row], sx.at[row], sx_s, sx_r.at[0 if kind == 0 else 1], x_left if kind == 1 else x_right
+        )
 
     def place_snapshot():
         snap_in.wait()
@@ -185,7 +200,7 @@
         snap_x(1).start()
 
     def snapshot_near():
-        snap_x_arrival(0).wait_recv()
+        received(sx.at[xl], sx_r.at[0])
         snap_x(2).start()
 
     def pass_token(t):
@@ -197,19 +212,9 @@
     def barrier_wait():
         pl.semaphore_wait(barrier, len(peers))
 
-    def spread_start(buf, own, peer_list, send, recv, src=None):
-        for index, peer in peer_list:
-            source = buf.at[own] if src is None else src.at[index]
-            remote(source, buf.at[own], send.at[index], recv.at[own], peer).start()
-
-    def spread_wait(buf, own, peer_list, send, recv):
-        for index, peer in peer_list:
-            remote(buf.at[index], buf.at[index], send.at[index], recv.at[index], peer).wait_recv()
-
-    def spread_done(buf, own, peer_list, send, recv, src=None):
-        for index, peer in peer_list:
-            source = buf.at[own] if src is None else src.at[index]
-            remote(source, buf.at[own], send.at[index], recv.at[own], peer).wait_send()
+    def spread_start(buf, own, peer_list, send, recv):
+        for _, peer in peer_list:
+            remote(buf.at[own], buf.at[own], send, recv, peer).start()
 
     def total(buf, count):
         result = buf[0]
@@ -217,73 +222,32 @@
             result = result + buf[index]
         return result
 
-    first = pl.ds(0, 2 * ZH)
-    halves = (pl.ds(0, ZH), pl.ds(ZH, ZH))
-    final = pl.ds(2 * ZH, VR)
+    halves = (pl.ds(0, AH), pl.ds(AH, AH))
 
     def z_copy(direction, slab):
-        ref = wp.at[c, slab, y, first]
+        ref = wp.at[c, slab, y]
         return remote(
-            ref, ref, agz_s.at[direction, slab], agz_r.at[direction, slab], up_two if direction == 0 else down_two
+            ref, ref, agz_s.at[direction, slab // 2], agz_r.at[slab // 2], up_two if direction == 0 else down_two
         )
 
     def mate_copy(slab):
-        ref = wp.at[c, slab, y, first]
-        return remote(ref, ref, agp_s.at[slab], agp_r.at[slab], mate)
-
-    def v_copy(direction, slab, yy):
-        ref = wp.at[c, slab, yy, final]
-        return remote(
-            ref, ref, agv_s.at[direction, slab, yy], agv_r.at[direction, slab, yy], up if direction == 0 else down
-        )
+        ref = wp.at[c, slab, y]
+        return remote(ref, ref, agp_s, agp_r.at[slab // 2], mate)
 
     def y_copy(kind, slab):
         device = right if kind in (0, 2) else left
         if kind < 2:
-            ref = wp.at[c, slab, y, first]
+            ref = wp.at[c, slab, y]
         elif kind == 2:
             ref = wp.at[c, slab, yl, halves[0]]
         else:
             ref = wp.at[c, slab, yr, halves[1]]
-        return remote(ref, ref, ay_s.at[kind, slab], ay_r.at[kind, slab], device)
-
-    def y_arrival(kind, slab):
-        ref = [
-            wp.at[c, slab, yl, first], wp.at[c, slab, yr, first], wp.at[c, slab, yo, halves[0]],
-            wp.at[c, slab, yo, halves[1]],
-        ][kind]
-        return remote(ref, ref, ay_s.at[kind, slab], ay_r.at[kind, slab], right)
+        return remote(ref, ref, ay_s, ay_r.at[kind // 2, slab], device)
 
     low, high = pl.ds(0, VH), pl.ds(VH, VH)
-    final_low, final_high = pl.ds(2 * ZH, VH), pl.ds(2 * ZH + VH, VH)
-
-    def vy_copy(kind):
-        device = right if kind in (0, 2) else left
-        if kind < 2:
-            ref = wp.at[c, z, y, final]
-        elif kind == 2:
-            ref = wp.at[c, z, yl, final_low]
-        else:
-            ref = wp.at[c, z, yr, final_high]
-        return remote(ref, ref, av_s.at[kind], av_r.at[kind], device)
-
-    def vy_arrival(kind):
-        ref = [
-            wp.at[c, z, yl, final], wp.at[c, z, yr, final], wp.at[c, z, yo, final_low], wp.at[c, z, yo, final_high],
-        ][kind]
-        return remote(ref, ref, av_s.at[kind], av_r.at[kind], right)
 
     def twin_copy(slab, core):
-        return remote(wp.at[core, slab], wp.at[core, slab], tw_s.at[slab], tw_r.at[slab], twin)
-
-    def both_ways(send):
-        @pl.when(z < NZ - 1)
-        def _():
-            send(0)
-
-        @pl.when(z > 0)
-        def _():
-            send(1)
+        return remote(wp.at[core, slab], wp.at[core, slab], tw_s, tw_r.at[slab], twin)
 
     def both_ways_two(send):
         @pl.when(pair < pairs - 1)
@@ -295,28 +259,10 @@
             send(1)
 
     def gather_own():
-        vy_copy(0).start()
-        vy_copy(1).start()
         both_ways_two(lambda direction: z_copy(direction, z).start())
-        mate_copy(z).start()
-        both_ways(lambda direction: v_copy(direction, z, y).start())
         y_copy(0, z).start()
         y_copy(1, z).start()
-
-    def gather_near():
-        vy_arrival(0).wait_recv()
-        vy_copy(2).start()
-        both_ways(lambda direction: v_copy(direction, z, yl).start())
-        vy_arrival(1).wait_recv()
-        vy_copy(3).start()
-        both_ways(lambda direction: v_copy(direction, z, yr).start())
-
-    def gather_far():
-        vy_arrival(2).wait_recv()
-        vy_arrival(3).wait_recv()
-        both_ways(lambda direction: v_copy(direction, z, yo).start())
-
-    v_order = (y, yl, yr, yo)
+        mate_copy(z).start()
 
     def gather_z(t):
         for direction, slab, here, more in (
@@ -343,28 +289,15 @@
                 y_copy(0, slab).start()
                 y_copy(1, slab).start()
 
-    def gather_v(t):
-        for direction, slab, here, more in ((0, z - t, z - t >= 0, z < NZ - 1), (1, z + t, z + t <= NZ - 1, z > 0)):
-            @pl.when(here)
-            def _():
-                for yy in v_order:
-                    v_copy(direction, slab, yy).wait_recv()
-
-                    @pl.when(more)
-                    def _():
-                        v_copy(direction, slab, yy).start()
-
     def gather_y(j):
         slab = order(z, 7 - j)
-        y_arrival(0, slab).wait_recv()
+        received(wp.at[c, slab, pl.ds(0, 2)], ay_r.at[0, slab])
         y_copy(2, slab).start()
-        y_arrival(1, slab).wait_recv()
         y_copy(3, slab).start()
 
     def gather_twin(j):
         slab = order(z, 7 - j)
-        y_arrival(2, slab).wait_recv()
-        y_arrival(3, slab).wait_recv()
+        received(wp.at[c, slab, yo], ay_r.at[1, slab])
         twin_copy(slab, c).start()
 
     def unpack(lo, hi):
@@ -411,10 +344,10 @@
 
     def nx_nb(core, half):
         ref = nbx.at[core, pl.ds(half * TOK // 2, TOK // 2)]
-        return remote(ref, ref, nx_s.at[half], nx_r.at[half], twin)
+        return remote(ref, ref, nx_s.at[0], nx_r.at[0], twin)
 
     def nx_gv(core):
-        return remote(gx.at[core], gx.at[core], nx_s.at[2], nx_r.at[2], twin)
+        return remote(gx.at[core], gx.at[core], nx_s.at[1], nx_r.at[1], twin)
 
     def weight_terms(core, lo, hi):
         columns = pl.ds(pl.multiple_of(HALF * c, 128), HALF)
@@ -441,23 +374,23 @@
 
     def far_copy(kind, slab):
         return remote(
-            s1.at[slab, kind], r1.at[slab, kind], ry_s.at[kind, slab], ry_r.at[kind, slab], right if kind == 0 else left
+            s1.at[slab, kind], r1.at[slab, kind], ry_s.at[0], ry_r.at[0, slab], right if kind == 0 else left
         )
 
     def near_copy(kind, slab):
         return remote(
-            s2.at[slab, kind], r2.at[slab, kind], ry_s.at[2 + kind, slab], ry_r.at[2 + kind, slab],
+            s2.at[slab, kind], r2.at[slab, kind], ry_s.at[1], ry_r.at[1, slab],
             right if kind == 0 else left,
         )
 
     def chain_copy(direction, slab):
         return remote(
-            sz.at[slab], rz.at[direction, slab], rz_s.at[direction, slab], rz_r.at[direction, slab],
+            sz.at[slab], rz.at[direction, slab], rz_s, rz_r.at[direction, slab // 2],
             up_two if direction == 0 else down_two,
         )
 
     def pair_copy(slab):
-        return remote(sp.at[slab // 2], rp.at[slab // 2], rp_s.at[slab // 2], rp_r.at[slab // 2], mate)
+        return remote(sp.at[slab // 2], rp.at[slab // 2], rp_s, rp_r.at[slab // 2], mate)
 
     def reduce_pair(i):
         slab = order(z, 2 * i)
@@ -469,10 +402,9 @@
         pair_copy(slab).wait_recv()
         racc[slab] = racc[slab] + rp[slab // 2].astype(F32)
 
-    def chain_v_copy(direction, slab, yy):
+    def chain_v_copy(direction, slab):
         return remote(
-            vz.at[slab, yy], rv.at[direction, slab, yy], rv_s.at[direction, slab, yy], rv_r.at[direction, slab, yy],
-            up if direction == 0 else down,
+            vz.at[slab], rv.at[direction, slab], rv_s, rv_r.at[direction, slab], up if direction == 0 else down
         )
 
     def reduce_far(s):
@@ -483,16 +415,15 @@
 
     def reduce_near(s):
         slab = order(z, s)
+        received(r1.at[slab], ry_r.at[0, slab])
         for kind, yy in ((0, yr), (1, yl)):
-            far_copy(kind, slab).wait_recv()
             s2[slab, kind, kind] = (term(slab, yy, ZH * kind, ZH) + r1[slab, kind].astype(F32)).astype(BF16)
             s2[slab, kind, 1 - kind] = term(slab, yy, ZH * (1 - kind), ZH).astype(BF16)
             near_copy(kind, slab).start()
 
     def reduce_row(s):
         slab = order(z, s)
-        near_copy(0, slab).wait_recv()
-        near_copy(1, slab).wait_recv()
+        received(r2.at[slab], ry_r.at[1, slab])
         for p in range(2):
             racc[slab, p] = term(slab, y, ZH * p, ZH) + r2[slab, 0, p].astype(F32) + r2[slab, 1, p].astype(F32)
 
@@ -526,13 +457,17 @@
 
     def reduce_v(u):
         if u == NZ - 1:
+            for direction, here in ((0, z > 0), (1, z < NZ - 1)):
+                @pl.when(here)
+                def _():
+                    chain_v_copy(direction, z).wait_recv()
+
             for k in (2, 1, 3, 0):
                 yy = (y + k) % NY
                 vacc[k] = term(z, yy, 2 * ZH, VR)
                 for direction, here in ((0, z > 0), (1, z < NZ - 1)):
                     @pl.when(here)
                     def _():
-                        chain_v_copy(direction, z, yy).wait_recv()
                         vacc[k] = vacc[k] + rv[direction, z, yy].astype(F32)
 
                 if k == 2:
@@ -546,61 +481,67 @@
         ):
             @pl.when(here)
             def _():
-                for k in (2, 1, 3, 0):
-                    yy = (y + k) % NY
-
-                    @pl.when(later)
-                    def _():
-                        chain_v_copy(direction, slab, yy).wait_recv()
+                @pl.when(later)
+                def _():
+                    chain_v_copy(direction, slab).wait_recv()
+                    for yy in range(NY):
                         vz[slab, yy] = (term(slab, yy, 2 * ZH, VR) + rv[direction, slab, yy].astype(F32)).astype(BF16)
 
-                    @pl.when(jnp.logical_not(later))
-                    def _():
+                @pl.when(jnp.logical_not(later))
+                def _():
+                    for yy in range(NY):
                         vz[slab, yy] = term(slab, yy, 2 * ZH, VR).astype(BF16)
 
-                    chain_v_copy(direction, slab, yy).start()
+                chain_v_copy(direction, slab).start()
 
     def v_far(kind):
         part = low if kind == 0 else high
-        return remote(vs1.at[part], vr1.at[part], vy_s.at[kind], vy_r.at[kind], right if kind == 0 else left)
+        return remote(vs1.at[part], vr1.at[part], vy_s.at[0], vy_r.at[0], right if kind == 0 else left)
 
     def v_near(kind):
-        return remote(vs2.at[kind], vr2.at[kind], vy_s.at[2 + kind], vy_r.at[2 + kind], right if kind == 0 else left)
+        return remote(vs2.at[kind], vr2.at[kind], vy_s.at[1], vy_r.at[1], right if kind == 0 else left)
 
     def reduce_v_near():
-        v_far(0).wait_recv()
+        received(vr1, vy_r.at[0])
         vs2[0] = jnp.concatenate(
             [vacc[1, 0:VH] + vr1[0:VH].astype(F32), vacc[1, VH:VR]], axis=0
         ).astype(BF16)
         v_near(0).start()
-        v_far(1).wait_recv()
         vs2[1] = jnp.concatenate(
             [vacc[3, 0:VH], vacc[3, VH:VR] + vr1[VH:VR].astype(F32)], axis=0
         ).astype(BF16)
         v_near(1).start()
 
     def reduce_v_row():
-        v_near(0).wait_recv()
-        v_near(1).wait_recv()
+        received(vr2, vy_r.at[1])
         fbuf[c, 2 * ZH : BLOCK] = vacc[0] + vr2[0].astype(F32) + vr2[1].astype(F32)
 
-    def make_values():
+    near_half, far_half = z // 4, 1 - z // 4
+
+    def make_values(half, done):
+        feats = pl.ds(pl.multiple_of(D // 2 * half, 128), D // 2)
+
         def one(n, _):
             columns = pl.ds(pl.multiple_of(256 * n, 256), 256)
-            vout[:, columns] = (jnp.dot(nbg[...], w[:, columns], preferred_element_type=F32) * FACTOR).astype(BF16)
+            part = jnp.dot(nbg[:, feats], w[feats, columns], preferred_element_type=F32)
+            if done:
+                vout[:, columns] = ((vf[:, columns] + part) * FACTOR).astype(BF16)
+            else:
+                vf[:, columns] = part
             return 0
 
         lax.fori_loop(0, KV // 256, one, 0)
 
-    def input_gradient(lo, hi):
+    def input_gradient(half):
         def one(k, _):
-            feats = pl.ds(pl.multiple_of(256 * k, 256), 256)
-            ig[:, feats] = (
-                lax.dot_general(gx[c], w[feats, :], (((1,), (1,)), ((), ())), preferred_element_type=F32) * FACTOR
-            )
+            feats = pl.ds(pl.multiple_of(D // 2 * half + 384 * k, 128), 384)
+            grad = lax.dot_general(gx[c], w[feats, :], (((1,), (1,)), ((), ())), preferred_element_type=F32) * FACTOR
+            ig[:, feats] = grad
+            normed = hid[:, feats].astype(F32) * invb[:, 0:1]
+            gacc[:, feats] = jnp.sum((grad * normed).reshape(TOK // 8, 8, 384), axis=0)
             return 0
 
-        lax.fori_loop(lo, hi, one, 0)
+        lax.fori_loop(0, D // 2 // 384, one, 0)
 
     def hidden_gradient(lo, hi):
         def one(r, _):
@@ -609,7 +550,6 @@
             normed = hid[rows, :].astype(F32) * inverse
             grad = ig[rows, :]
             along = grad * normed
-            gacc[...] += jnp.sum(along.reshape(4, 8, D), axis=0)
             gain = grow[0:1, :]
             mean = jnp.sum(along * gain, axis=-1, keepdims=True) / D
             gh[rows, :] = (inverse * (grad * gain - normed * mean)).astype(BF16)
@@ -617,23 +557,28 @@
 
         lax.fori_loop(lo, hi, one, 0)
 
-    def gain_terms():
-        gain_row = jnp.sum(gacc[...], axis=0, keepdims=True)
-        hsrc[...] = jnp.zeros((NZ, 8, 128), F32)
-        for slab in range(NZ):
-            for r in range(3):
-                lanes = slice(128 * (window_start(slab) + r), 128 * (window_start(slab) + r + 1))
-                hsrc[slab, r : r + 1, :] = gain_row[:, lanes]
+    def gain_terms(half):
+        for side in range(2):
+            @pl.when(half == side)
+            def _():
+                for slab in range(4 * side, 4 * side + 4):
+                    hsrc[slab] = jnp.zeros((8, 128), F32)
+                    for r in range(3):
+                        lanes = slice(128 * (window_start(slab) + r), 128 * (window_start(slab) + r + 1))
+                        hsrc[slab, r : r + 1, :] = jnp.sum(gacc[:, lanes], axis=0, keepdims=True)
+
+                    @pl.when(z != slab)
+                    def _():
+                        remote(hsrc.at[slab], h1.at[z], h1_s, h1_r, (g, slab * NE + e)).start()
+
+    def gain_second():
+        received(h1.at[pl.ds(0, NZ - 1)], h1_r)
         h1[z] = hsrc[z]
-        spread_start(h1, z, z_peers, h1_s, h1_r, src=hsrc)
-
-    def gain_second():
-        spread_wait(h1, z, z_peers, h1_s, h1_r)
         h2[e] = total(h1, NZ)
         spread_start(h2, e, e_peers, h2_s, h2_r)
 
     def gain_step():
-        spread_wait(h2, e, e_peers, h2_s, h2_r)
+        received(h2.at[pl.ds(0, NE - 1)], h2_r)
         window = total(h2, NE)
         gain_grad = jnp.zeros((8, ROWS), F32)
         for r in range(3):
@@ -646,8 +591,7 @@
         out(3).start()
 
     def snapshot_second():
-        snap_x_arrival(1).wait_recv()
-        snap_x_arrival(2).wait_recv()
+        received(sx.at[pl.ds(0, 2)], sx_r.at[1])
         szh[zh] = total(sx, NX)
         szh_copy(zh).start()
 
@@ -694,17 +638,11 @@
     def out(index):
         return pltpu.make_async_copy(results[index][0], results[index][1], out_sem.at[index])
 
+    def results_wait():
+        for index in range(6):
+            out(index).wait()
+
     def drain():
-        for t in range(NZ):
-            for direction, slab, here in (
-                (0, z - t, jnp.logical_and(z - t >= 0, z < NZ - 1)), (1, z + t, jnp.logical_and(z + t <= NZ - 1, z > 0)),
-            ):
-                @pl.when(here)
-                def _():
-                    gain_z(direction, slab).wait_send()
-                    for yy in range(NY):
-                        v_copy(direction, slab, yy).wait_send()
-
         for t in range(pairs):
             for direction, slab, here in (
                 (0, z - 2 * t, jnp.logical_and(pair >= t, pair < pairs - 1)),
@@ -713,58 +651,34 @@
                 @pl.when(here)
                 def _():
                     z_copy(direction, slab).wait_send()
-
-        def one(slab, _):
-            for kind in range(4):
-                y_copy(kind, slab).wait_send()
-            twin_copy(slab, c).wait_send()
-            for kind in range(2):
-                far_copy(kind, slab).wait_send()
-                near_copy(kind, slab).wait_send()
-
-            for direction, here in ((0, slab > z), (1, slab < z)):
-                @pl.when(here)
-                def _():
-                    for yy in range(NY):
-                        chain_v_copy(direction, slab, yy).wait_send()
-
-                @pl.when(jnp.logical_and(here, slab % 2 == z % 2))
-                def _():
-                    chain_copy(direction, slab).wait_send()
-
-            @pl.when(slab % 2 == z % 2)
-            def _():
-                mate_copy(slab).wait_send()
-
-            @pl.when(slab % 2 != z % 2)
-            def _():
-                pair_copy(slab).wait_send()
-
-            return 0
-
-        lax.fori_loop(0, NZ, one, 0)
-        for kind in range(4):
-            vy_copy(kind).wait_send()
-        for kind in range(2):
-            v_far(kind).wait_send()
-            v_near(kind).wait_send()
-        nx_nb(c, 0).wait_send()
-        nx_nb(c, 1).wait_send()
-        nx_gv(c).wait_send()
-        last(c).wait_send()
-        szh_copy(zh).wait_send()
-        gain_twin(c).wait_send()
-        for kind in range(3):
-            gain_y(kind).wait_send()
-            snap_x(kind).wait_send()
-        spread_done(h1, z, z_peers, h1_s, h1_r, src=hsrc)
+                    gain_z(direction, slab).wait_send()
+
+        sent(wp.at[0, 0], agp_s)
+        sent(wp.at[0, pl.ds(0, 6)], ay_s)
+        sent(wp.at[0], tw_s)
+        sent(s1, ry_s.at[0])
+        sent(s2, ry_s.at[1])
+        sent(sp, rp_s)
+        sent(sz.at[pl.ds(0, pairs - 1)], rz_s)
+        sent(vz.at[pl.ds(0, NZ - 1)], rv_s)
+        sent(vs1, vy_s.at[0])
+        sent(vs2, vy_s.at[1])
+        sent(nbx.at[0], nx_s.at[0])
+        sent(gx.at[0], nx_s.at[1])
+        sent(fbuf.at[0], f_s)
+        sent(szh.at[0], szh_s)
+        sent(g0.at[0], g0_s)
+        sent(g1.at[pl.ds(0, 3)], g1_s)
+        sent(g2.at[pl.ds(0, pairs)], gm_s)
+        sent(sx.at[pl.ds(0, 3)], sx_s)
+        sent(hsrc.at[pl.ds(0, NZ - 1)], h1_s)
+        sent(h2.at[pl.ds(0, NE - 1)], h2_s)
 
     place_gains()
     pack_own()
     barrier_wait()
     gain_twin(c).start()
     gather_own()
-    pass_token(0)
     gv_in.wait()
     nx_gv(c).start()
     hid_in.wait()
@@ -774,129 +688,115 @@
     nx_nb(c, 1).start()
     gain_chip()
     place_snapshot()
-    gather_near()
     weight_terms(c, 0, 5)
-    gather_far()
+    weight_terms(c, 5, 9)
+    gain_near()
+    gather_y(0)
     gather_mate(0)
+    nx_gv(1 - c).wait_recv()
+    received(nbx.at[1 - c], nx_r.at[0])
+    weight_terms(1 - c, 0, 5)
     gather_z(1)
-    weight_terms(c, 5, 9)
-    gather_v(1)
-    gather_y(0)
-    pass_token(1)
-    gain_near()
-    nx_gv(1 - c).wait_recv()
-    nx_nb(1 - c, 0).wait_recv()
-    nx_nb(1 - c, 1).wait_recv()
-    weight_terms(1 - c, 0, 5)
-    gather_y(1)
-    gather_mate(1)
     weight_terms(1 - c, 5, 9)
-    gather_z(2)
-    gather_v(2)
     reduce_v(0)
+    pass_token(0)
     reduce_far(0)
     reduce_far(1)
     gain_slab()
+    gather_y(1)
+    gather_twin(0)
+    gather_mate(1)
+    gather_z(2)
     snapshot_near()
-    pass_token(2)
-    gather_v(3)
-    gather_y(2)
-    gather_mate(2)
-    gather_twin(0)
     reduce_v(1)
-    gather_z(3)
-    gather_y(3)
-    gather_twin(1)
+    pass_token(1)
     reduce_near(0)
     reduce_near(1)
+    gather_y(2)
+    gather_gain(1)
+    gather_mate(2)
+    gather_twin(1)
+    reduce_v(2)
+    gather_y(3)
+    gather_z(3)
+    pass_token(2)
     reduce_far(2)
     reduce_far(3)
+    gather_twin(2)
+    gather_gain(2)
+    gather_y(4)
+    reduce_v(3)
+    gather_mate(3)
+    gather_twin(3)
     pass_token(3)
-    gather_gain(1)
-    gather_v(4)
-    reduce_v(2)
-    gather_mate(3)
-    gather_y(4)
-    gather_twin(2)
+    gather_y(5)
     reduce_row(0)
     reduce_row(1)
     reduce_pair(0)
     reduce_near(2)
     reduce_near(3)
+    gather_gain(3)
+    reduce_v(4)
+    gather_twin(4)
+    gather_y(6)
+    unpack(0, 4)
     pass_token(4)
-    gather_gain(2)
-    gather_v(5)
-    reduce_v(3)
-    gather_y(5)
-    gather_twin(3)
     reduce_far(4)
     reduce_far(5)
     reduce_chain(0)
+    input_gradient(near_half)
+    gain_terms(near_half)
     pass_token(5)
-    gather_gain(3)
-    gather_v(6)
-    reduce_v(4)
-    gather_y(6)
-    gather_twin(4)
-    unpack(0, 2)
+    gather_twin(5)
+    gather_y(7)
+    reduce_v(5)
     reduce_row(2)
     reduce_row(3)
     reduce_pair(1)
     reduce_near(4)
     reduce_near(5)
+    pass_token(6)
     reduce_far(6)
     reduce_far(7)
-    pass_token(6)
-    gather_gain(4)
-    gather_v(7)
-    gather_y(7)
-    gather_twin(5)
-    reduce_v(5)
+    gather_twin(6)
+    gather_twin(7)
+    reduce_v(6)
     reduce_chain(1)
     pass_token(7)
     snapshot_second()
-    gather_twin(6)
-    unpack(2, 4)
+    gain_all()
+    gain_vector()
+    unpack(4, 6)
     reduce_row(4)
     reduce_row(5)
     reduce_pair(2)
     reduce_near(6)
     reduce_near(7)
-    gather_gain(5)
-    gather_twin(7)
-    reduce_v(6)
-    gather_gain(6)
-    unpack(4, 6)
-    reduce_chain(2)
-    gather_gain(7)
-    gain_vector()
+    unpack(6, 8)
+    input_gradient(far_half)
+    gain_terms(far_half)
     reduce_v(7)
     apply_gain()
     reduce_row(6)
     reduce_row(7)
     reduce_pair(3)
-    unpack(6, 8)
-    input_gradient(0, 5)
     reduce_v_near()
-    input_gradient(5, 9)
+    reduce_chain(2)
+    make_values(near_half, False)
+    hidden_gradient(0, 8)
+    out(1).start()
+    reduce_v_row()
     reduce_chain(3)
     fbuf[c, 0 : 2 * ZH] = racc[z].reshape(2 * ZH, 128)
-    gacc[...] = jnp.zeros((8, D), F32)
-    hidden_gradient(0, 8)
-    out(1).start()
-    gain_terms()
-    reduce_v_row()
     last(c).start()
-    make_values()
+    gain_second()
+    make_values(far_half, True)
     out(0).start()
     outer_step()
     inner_step()
-    gain_second()
     drain()
     gain_step()
-    spread_done(h2, e, e_peers, h2_s, h2_r)
-    for index in range(6):
-        out(index).wait()
+    results_wait()
 
 
 def place_kernel(*refs):
@@ -957,6 +857,7 @@
             vmem((2, NZ, NY, VR, 128), BF16),
             vmem((2, BLOCK, 128), F32),
             vmem((TOK, D), F32),
+            vmem((TOK, KV), F32),
             vmem((TOK, KV), BF16),
             vmem((TOK, D), BF16),
             vmem((TOK, 128), F32),
@@ -980,30 +881,26 @@
             vmem((ROWS, FW), F32),
             vmem((ROWS, FW), F32),
             dma((7,)), dma((6,)),
-            dma((2, NZ)), dma((2, NZ)),
-            dma((NZ,)), dma((NZ,)),
-            dma((2, NZ, NY)), dma((2, NZ, NY)),
-            dma((4, NZ)), dma((4, NZ)),
-            dma((4,)), dma((4,)),
-            dma((NZ,)), dma((NZ,)),
-            dma((3,)), dma((3,)),
-            dma((4, NZ)), dma((4, NZ)),
-            dma((NZ // 2,)), dma((NZ // 2,)),
-            dma((2, NZ)), dma((2, NZ)),
-            dma((2, NZ, NY)), dma((2, NZ, NY)),
-            dma((4,)), dma((4,)),
+            dma((2, NZ // 2)), dma((NZ // 2,)), dma, dma((NZ // 2,)),
+            dma, dma((2, NZ)),
+            dma, dma((NZ,)),
+            dma((2,)), dma((2,)),
+            dma((2,)), dma((2, NZ)),
+            dma, dma((NZ // 2,)),
+            dma, dma((2, NZ // 2)),
+            dma, dma((2, NZ)),
+            dma((2,)), dma((2,)),
             dma, dma,
             dma, dma,
-            dma((3,)), dma((3,)),
-            dma((2, NZ)), dma((2, NZ)),
-            dma((NZ,)), dma((NZ,)),
-            dma((NE,)), dma((NE,)),
-            dma((3,)), dma((3,)),
+            dma, dma((2,)),
+            dma((2, NZ // 2)), dma((NZ // 2,)), dma, dma,
+            dma, dma, dma, dma,
+            dma, dma((2,)),
             dma, dma,
             pltpu.SemaphoreType.REGULAR((7,)),
         ],
         compiler_params=pltpu.CompilerParams(
-            collective_id=0, has_side_effects=True, vmem_limit_bytes=56 * 1024 * 1024
+            collective_id=0, has_side_effects=True, vmem_limit_bytes=56 * 1024 * 1024,
         ),
         cost_estimate=pl.CostEstimate(flops=3 * 2 * TOK * D * KV, bytes_accessed=4_000_000, transcendentals=0),
     )(

time: 80.9 us -> 71 us (0.88)
  Pallas kernels: 79.4 us -> 69.5 us
    pallas_call x1, Pallas kernels: 76.8 us -> 66.9 us  [body(): pl.pallas_call(step_kernel, out_shape=shapes, in_specs=[pl.BlockSpec(memo...]
where the time goes in v3:
time: 71 us; the launch traced here: 70.8 us
  Pallas kernels  69.5 us (98%)
  between operations  1.29 us (2%)
    pallas_call x1, Pallas kernels, body(): pl.pallas_call(step_kernel, out_shape=shapes, in_specs=[pl.BlockSpec(memo...  66.9 us
    pallas_call x1, Pallas kernels, body(): pl.pallas_call(place_kernel, out_shape=shapes, in_specs=[anywhere] * 6, o...  2.6 us

profile of v3, /device:TPU:1, one launch (start us, length us, event | category | flops | bytes accessed | tf_op | source)
XLA Modules:
  0.0 70.8 jit_solution(5985956647981742915)
XLA Ops:
  1.3 66.9 %shard_map.127 = (bf16[256,1024]{1,0:T(8,128)(2,1)}, bf16[256,2304]{1,0:T(8,128)(2,1)}, f32[288,128]{1,0:T(8,128)}, f32[1,36]{1,0:T(1,128)}, f32[36,128]{1,0:T(8,128)}, /*index=5*/f32[36,128]{1,0:T(8,128)}) custom-call(s32[1]{0:T(128)S(6)} %copy.16.frag_ref, bf16[256,2304]{1,0:T(8,128)(2,1)} %hid_hbm.1, bf16[256,1024]{1,0:T(8,128)(2,1)} %gv_hbm.1, ...), custom_call_target="tpu_custom_call" | custom-call | flops 3623878656 | bytes 4000000 | tf_op jit(solution)/shard_map/pallas_call | solution.py:827
  68.2 2.6 %shard_map.128 = (bf16[256,1024]{1,0:T(8,128)(2,1)}, bf16[256,2304]{1,0:T(8,128)(2,1)}, f32[288,128]{1,0:T(8,128)}, f32[1,36]{1,0:T(1,128)}, f32[36,128]{1,0:T(8,128)}, /*index=5*/f32[36,128]{1,0:T(8,128)}) custom-call(bf16[256,1024]{1,0:T(8,128)(2,1)} %get-tuple-element.18.refs_0_, bf16[256,2304]{1,0:T(8,128)(2,1)} %get-tuple-element.19.refs_1_, ...), custom_call_target="tpu_custom_call" | custom-call | tf_op jit(solution)/shard_map/pallas_call | solution.py:910

commit v4 on v3

--- a/solution.py
+++ b/solution.py
@@ -679,6 +679,7 @@
     barrier_wait()
     gain_twin(c).start()
     gather_own()
+    pass_token(0)
     gv_in.wait()
     nx_gv(c).start()
     hid_in.wait()
@@ -697,11 +698,12 @@
     received(nbx.at[1 - c], nx_r.at[0])
     weight_terms(1 - c, 0, 5)
     gather_z(1)
+    pass_token(1)
     weight_terms(1 - c, 5, 9)
     reduce_v(0)
-    pass_token(0)
     reduce_far(0)
     reduce_far(1)
+    pass_token(2)
     gain_slab()
     gather_y(1)
     gather_twin(0)
@@ -709,17 +711,18 @@
     gather_z(2)
     snapshot_near()
     reduce_v(1)
-    pass_token(1)
+    pass_token(3)
     reduce_near(0)
     reduce_near(1)
     gather_y(2)
     gather_gain(1)
     gather_mate(2)
+    pass_token(4)
     gather_twin(1)
     reduce_v(2)
     gather_y(3)
     gather_z(3)
-    pass_token(2)
+    pass_token(5)
     reduce_far(2)
     reduce_far(3)
     gather_twin(2)
@@ -728,44 +731,43 @@
     reduce_v(3)
     gather_mate(3)
     gather_twin(3)
-    pass_token(3)
+    pass_token(6)
     gather_y(5)
     reduce_row(0)
     reduce_row(1)
     reduce_pair(0)
     reduce_near(2)
     reduce_near(3)
+    pass_token(7)
+    snapshot_second()
     gather_gain(3)
     reduce_v(4)
     gather_twin(4)
     gather_y(6)
     unpack(0, 4)
-    pass_token(4)
     reduce_far(4)
     reduce_far(5)
     reduce_chain(0)
     input_gradient(near_half)
     gain_terms(near_half)
-    pass_token(5)
     gather_twin(5)
     gather_y(7)
     reduce_v(5)
     reduce_row(2)
     reduce_row(3)
     reduce_pair(1)
+    gain_all()
+    gain_vector()
+    apply_gain()
     reduce_near(4)
     reduce_near(5)
-    pass_token(6)
     reduce_far(6)
     reduce_far(7)
     gather_twin(6)
     gather_twin(7)
+    make_values(near_half, False)
     reduce_v(6)
     reduce_chain(1)
-    pass_token(7)
-    snapshot_second()
-    gain_all()
-    gain_vector()
     unpack(4, 6)
     reduce_row(4)
     reduce_row(5)
@@ -776,33 +778,34 @@
     input_gradient(far_half)
     gain_terms(far_half)
     reduce_v(7)
-    apply_gain()
     reduce_row(6)
+    reduce_pair(3)
     reduce_row(7)
-    reduce_pair(3)
+    reduce_chain(2)
     reduce_v_near()
-    reduce_chain(2)
-    make_values(near_half, False)
     hidden_gradient(0, 8)
     out(1).start()
+    gain_second()
     reduce_v_row()
     reduce_chain(3)
     fbuf[c, 0 : 2 * ZH] = racc[z].reshape(2 * ZH, 128)
     last(c).start()
-    gain_second()
     make_values(far_half, True)
     out(0).start()
     outer_step()
+    drain()
     inner_step()
-    drain()
     gain_step()
     results_wait()
 
 
 def place_kernel(*refs):
     sources, targets, held, in_sem, out_sem = refs[:6], refs[6:12], refs[12:18], refs[18], refs[19]
-    arrive = [pltpu.make_async_copy(s, t, in_sem.at[i]) for i, (s, t) in enumerate(zip(sources, held))]
-    leave = [pltpu.make_async_copy(s, t, out_sem.at[i]) for i, (s, t) in enumerate(zip(held, targets))]
+    slices = [(1, pl.ds(64 * k, 64)) for k in range(4)] + [(0, pl.ds(128 * k, 128)) for k in range(2)]
+    parts = [(s.at[rows], h.at[rows], t.at[rows]) for i, rows in slices for s, h, t in [(sources[i], held[i], targets[i])]]
+    parts += [(sources[i], held[i], targets[i]) for i in range(2, 6)]
+    arrive = [pltpu.make_async_copy(s, h, in_sem.at[k]) for k, (s, h, _) in enumerate(parts)]
+    leave = [pltpu.make_async_copy(h, t, out_sem.at[k]) for k, (_, h, t) in enumerate(parts)]
     for copy in arrive:
         copy.start()
     for one, other in zip(arrive, leave):
@@ -912,7 +915,7 @@
         out_shape=shapes,
         in_specs=[anywhere] * 6,
         out_specs=(anywhere,) * 6,
-        scratch_shapes=[vmem(shape.shape, shape.dtype) for shape in shapes] + [dma((6,)), dma((6,))],
+        scratch_shapes=[vmem(shape.shape, shape.dtype) for shape in shapes] + [dma((10,)), dma((10,))],
         compiler_params=pltpu.CompilerParams(vmem_limit_bytes=60 * 1024 * 1024),
     )(*results)
     return (values, grad_hidden, new_weights.reshape(1, ROWS, KV), new_gains, new_outer, new_moment)

time: 71 us -> 68.3 us (0.962)
  Pallas kernels: 69.5 us -> 66.9 us
    pallas_call x1, Pallas kernels: 66.9 us -> 64.5 us  [body(): pl.pallas_call(step_kernel, out_shape=shapes, in_specs=[pl.BlockSpec(memo...]
where the time goes in v4:
time: 68.3 us; the launch traced here: 68.2 us
  Pallas kernels  66.9 us (98%)
  between operations  1.29 us (2%)
    pallas_call x1, Pallas kernels, body(): pl.pallas_call(step_kernel, out_shape=shapes, in_specs=[pl.BlockSpec(memo...  64.5 us
    pallas_call x1, Pallas kernels, body(): pl.pallas_call(place_kernel, out_shape=shapes, in_specs=[anywhere] * 6, o...  2.37 us

profile of v4, /device:TPU:1, one launch (start us, length us, event | category | flops | bytes accessed | tf_op | source)
XLA Modules:
  0.0 68.2 jit_solution(4161521025721128561)
XLA Ops:
  1.3 64.5 %shard_map.127 = (bf16[256,1024]{1,0:T(8,128)(2,1)}, bf16[256,2304]{1,0:T(8,128)(2,1)}, f32[288,128]{1,0:T(8,128)}, f32[1,36]{1,0:T(1,128)}, f32[36,128]{1,0:T(8,128)}, /*index=5*/f32[36,128]{1,0:T(8,128)}) custom-call(s32[1]{0:T(128)S(6)} %copy.16.frag_ref, bf16[256,2304]{1,0:T(8,128)(2,1)} %hid_hbm.1, bf16[256,1024]{1,0:T(8,128)(2,1)} %gv_hbm.1, ...), custom_call_target="tpu_custom_call" | custom-call | flops 3623878656 | bytes 4000000 | tf_op jit(solution)/shard_map/pallas_call | solution.py:830
  65.8 2.4 %shard_map.128 = (bf16[256,1024]{1,0:T(8,128)(2,1)}, bf16[256,2304]{1,0:T(8,128)(2,1)}, f32[288,128]{1,0:T(8,128)}, f32[1,36]{1,0:T(1,128)}, f32[36,128]{1,0:T(8,128)}, /*index=5*/f32[36,128]{1,0:T(8,128)}) custom-call(bf16[256,1024]{1,0:T(8,128)(2,1)} %get-tuple-element.18.refs_0_, bf16[256,2304]{1,0:T(8,128)(2,1)} %get-tuple-element.19.refs_1_, ...), custom_call_target="tpu_custom_call" | custom-call | tf_op jit(solution)/shard_map/pallas_call | solution.py:913

commit v5 on v4

--- a/solution.py
+++ b/solution.py
@@ -518,11 +518,17 @@
 
     near_half, far_half = z // 4, 1 - z // 4
 
+    def last_values(core):
+        @pl.when(c == core)
+        def _():
+            make_values(far_half, True)
+            out(0).start()
+
     def make_values(half, done):
         feats = pl.ds(pl.multiple_of(D // 2 * half, 128), D // 2)
 
         def one(n, _):
-            columns = pl.ds(pl.multiple_of(256 * n, 256), 256)
+            columns = pl.ds(pl.multiple_of(512 * n, 512), 512)
             part = jnp.dot(nbg[:, feats], w[feats, columns], preferred_element_type=F32)
             if done:
                 vout[:, columns] = ((vf[:, columns] + part) * FACTOR).astype(BF16)
@@ -530,7 +536,7 @@
                 vf[:, columns] = part
             return 0
 
-        lax.fori_loop(0, KV // 256, one, 0)
+        lax.fori_loop(0, KV // 512, one, 0)
 
     def input_gradient(half):
         def one(k, _):
@@ -765,23 +771,22 @@
     reduce_far(7)
     gather_twin(6)
     gather_twin(7)
-    make_values(near_half, False)
     reduce_v(6)
     reduce_chain(1)
-    unpack(4, 6)
+    unpack(4, 8)
+    input_gradient(far_half)
+    gain_terms(far_half)
     reduce_row(4)
     reduce_row(5)
     reduce_pair(2)
     reduce_near(6)
     reduce_near(7)
-    unpack(6, 8)
-    input_gradient(far_half)
-    gain_terms(far_half)
     reduce_v(7)
+    make_values(near_half, False)
+    reduce_chain(2)
     reduce_row(6)
     reduce_pair(3)
     reduce_row(7)
-    reduce_chain(2)
     reduce_v_near()
     hidden_gradient(0, 8)
     out(1).start()
@@ -790,11 +795,11 @@
     reduce_chain(3)
     fbuf[c, 0 : 2 * ZH] = racc[z].reshape(2 * ZH, 128)
     last(c).start()
-    make_values(far_half, True)
-    out(0).start()
     outer_step()
+    last_values(1)
+    inner_step()
+    last_values(0)
     drain()
-    inner_step()
     gain_step()
     results_wait()
 

time: 68.3 us -> 67.7 us (level)
  Pallas kernels: 66.9 us -> 65.9 us
    pallas_call x1, Pallas kernels: 64.5 us -> 63.5 us  [body(): pl.pallas_call(step_kernel, out_shape=shapes, in_specs=[pl.BlockSpec(memo...]
where the time goes in v5:
time: 67.7 us; the launch traced here: 67.2 us
  Pallas kernels  65.9 us (97%)
  between operations  1.29 us (2%)
    pallas_call x1, Pallas kernels, body(): pl.pallas_call(step_kernel, out_shape=shapes, in_specs=[pl.BlockSpec(memo...  63.5 us
    pallas_call x1, Pallas kernels, body(): pl.pallas_call(place_kernel, out_shape=shapes, in_specs=[anywhere] * 6, o...  2.37 us

profile of v5, /device:TPU:1, one launch (start us, length us, event | category | flops | bytes accessed | tf_op | source)
XLA Modules:
  0.0 67.2 jit_solution(14089203605983780864)
XLA Ops:
  1.3 63.5 %shard_map.127 = (bf16[256,1024]{1,0:T(8,128)(2,1)}, bf16[256,2304]{1,0:T(8,128)(2,1)}, f32[288,128]{1,0:T(8,128)}, f32[1,36]{1,0:T(1,128)}, f32[36,128]{1,0:T(8,128)}, /*index=5*/f32[36,128]{1,0:T(8,128)}) custom-call(s32[1]{0:T(128)S(6)} %copy.16.frag_ref, bf16[256,2304]{1,0:T(8,128)(2,1)} %hid_hbm.1, bf16[256,1024]{1,0:T(8,128)(2,1)} %gv_hbm.1, ...), custom_call_target="tpu_custom_call" | custom-call | flops 3623878656 | bytes 4000000 | tf_op jit(solution)/shard_map/pallas_call | solution.py:835
  64.8 2.4 %shard_map.128 = (bf16[256,1024]{1,0:T(8,128)(2,1)}, bf16[256,2304]{1,0:T(8,128)(2,1)}, f32[288,128]{1,0:T(8,128)}, f32[1,36]{1,0:T(1,128)}, f32[36,128]{1,0:T(8,128)}, /*index=5*/f32[36,128]{1,0:T(8,128)}) custom-call(bf16[256,1024]{1,0:T(8,128)(2,1)} %get-tuple-element.18.refs_0_, bf16[256,2304]{1,0:T(8,128)(2,1)} %get-tuple-element.19.refs_1_, ...), custom_call_target="tpu_custom_call" | custom-call | tf_op jit(solution)/shard_map/pallas_call | solution.py:918

commit v6 on v5

--- a/solution.py
+++ b/solution.py
@@ -731,10 +731,10 @@
     pass_token(5)
     reduce_far(2)
     reduce_far(3)
+    reduce_v(3)
     gather_twin(2)
     gather_gain(2)
     gather_y(4)
-    reduce_v(3)
     gather_mate(3)
     gather_twin(3)
     pass_token(6)
@@ -742,12 +742,12 @@
     reduce_row(0)
     reduce_row(1)
     reduce_pair(0)
+    reduce_v(4)
     reduce_near(2)
     reduce_near(3)
     pass_token(7)
     snapshot_second()
     gather_gain(3)
-    reduce_v(4)
     gather_twin(4)
     gather_y(6)
     unpack(0, 4)

time: 67.7 us -> 67.1 us (level)
  no operation moved by 1% of the time
where the time goes in v6:
time: 67.1 us; the launch traced here: 66.9 us
  Pallas kernels  65.6 us (98%)
  between operations  1.29 us (2%)
    pallas_call x1, Pallas kernels, body(): pl.pallas_call(step_kernel, out_shape=shapes, in_specs=[pl.BlockSpec(memo...  63.2 us
    pallas_call x1, Pallas kernels, body(): pl.pallas_call(place_kernel, out_shape=shapes, in_specs=[anywhere] * 6, o...  2.37 us

profile of v6, /device:TPU:1, one launch (start us, length us, event | category | flops | bytes accessed | tf_op | source)
XLA Modules:
  0.0 66.9 jit_solution(5203171787618739284)
XLA Ops:
  1.3 63.2 %shard_map.127 = (bf16[256,1024]{1,0:T(8,128)(2,1)}, bf16[256,2304]{1,0:T(8,128)(2,1)}, f32[288,128]{1,0:T(8,128)}, f32[1,36]{1,0:T(1,128)}, f32[36,128]{1,0:T(8,128)}, /*index=5*/f32[36,128]{1,0:T(8,128)}) custom-call(s32[1]{0:T(128)S(6)} %copy.16.frag_ref, bf16[256,2304]{1,0:T(8,128)(2,1)} %hid_hbm.1, bf16[256,1024]{1,0:T(8,128)(2,1)} %gv_hbm.1, ...), custom_call_target="tpu_custom_call" | custom-call | flops 3623878656 | bytes 4000000 | tf_op jit(solution)/shard_map/pallas_call | solution.py:835
  64.5 2.4 %shard_map.128 = (bf16[256,1024]{1,0:T(8,128)(2,1)}, bf16[256,2304]{1,0:T(8,128)(2,1)}, f32[288,128]{1,0:T(8,128)}, f32[1,36]{1,0:T(1,128)}, f32[36,128]{1,0:T(8,128)}, /*index=5*/f32[36,128]{1,0:T(8,128)}) custom-call(bf16[256,1024]{1,0:T(8,128)(2,1)} %get-tuple-element.18.refs_0_, bf16[256,2304]{1,0:T(8,128)(2,1)} %get-tuple-element.19.refs_1_, ...), custom_call_target="tpu_custom_call" | custom-call | tf_op jit(solution)/shard_map/pallas_call | solution.py:918
